TPU v7x, 128 devices: a whole 4x4x4 slice. The times are simulated.
128 devices in a mesh: sub: 16 (over x, y), grp: 8 (over z, core).
Axes of the slice: x: 4, y: 4, z: 4, core: 2. Of those that a mesh axis runs over, the one named last changes fastest.
Arguments:
- res_inner: bfloat16 [8192, 16, 144], P(('sub', 'grp')), may hold values from -6 to 6
- res_face: bfloat16 [16384, 16, 144], P(('sub', 'grp')), may hold values from -6 to 6
- inner_inv: bfloat16 [8192, 144, 144], P(('sub', 'grp')), may hold values from -0.5 to 0.5
- face_coupling: bfloat16 [16384, 144, 144], P(('sub', 'grp')), may hold values from -0.5 to 0.5
- face_elem: int32 [128, 128], P(('sub', 'grp')), may hold values from 0 to 63
- face_inv: bfloat16 [16384, 144, 144], P(('sub', 'grp')), may hold values from -0.5 to 0.5
- coarse_basis: bfloat16 [16384, 64, 144], P(('sub', 'grp')), may hold values from -0.0625 to 0.0625
- coarse_map: int32 [128, 64], P(('sub', 'grp')), may hold values from 0 to 2047
- coarse_inv: float32 [2048, 2048], P('grp'), as said below
- recv_index: int32 [128, 128], P(('sub', 'grp')), may hold values from 0 to 32, as said below
- sharers: int32 [128, 128], P(('sub', 'grp')), may hold values from 0 to 128, as said below
Outputs:
- inner_out: bfloat16 [8192, 16, 144], P(('sub', 'grp'))
- face_out: bfloat16 [16384, 16, 144], P(('sub', 'grp'))
Inputs may be any that keep to these rules, and one draw needn't show every extreme that they name: `recv_index`: row o gives, for each subdomain s at position s, the index among the 32 blocks owned by subdomain o that slot o of subdomain s refers to, or 32 where that slot is unused. `sharers`: for a used slot, the number of used slots of all subdomains that refer to the same owned block, up to all 128 of them, which some block reaches; 0 exactly for unused slots. coarse_inv is symmetric.
All inputs are finite; a program needn't handle non-finite values.
Results may differ from a plain program's by a relative error of at most 0.006.
Values may be sent and summed in bfloat16 or wider, within the bound.
A program may use at most 128 MiB of HBM per device.

v0:
```python
import jax
import jax.numpy as jnp
from jax import lax
from jax.sharding import PartitionSpec as P


def cut_along(x, dim, size):
    before, after = (x.shape[:dim], x.shape[dim + 1 :])
    return jnp.moveaxis(x.reshape(*before, size, -1, *after), dim, 0)


def sum_at_owner(x, axis, dim):
    size = lax.axis_size(axis)
    blocks = lax.all_to_all(cut_along(x, dim, size), axis, 0, 0, tiled=True)
    return jnp.sum(blocks, axis=0)


def copy_for_each(x, axis):
    size = lax.axis_size(axis)
    return lax.all_to_all(jnp.broadcast_to(x[None], (size, *x.shape)), axis, 0, 0, tiled=True)


def over_copies(x, axis):
    everything = copy_for_each(x, axis)
    return jnp.sum(everything, axis=0)


def send_out(partials):
    return lax.all_to_all(partials, ("sub", "grp"), split_axis=0, concat_axis=0, tiled=True)


def send_back(spread):
    return lax.all_to_all(spread, ("sub", "grp"), split_axis=0, concat_axis=0, tiled=True)


def body(
    res_inner,
    res_face,
    inner_inv,
    face_coupling,
    face_elem,
    face_inv,
    coarse_basis,
    coarse_map,
    coarse_inv,
    recv_index,
    sharers,
):
    num_faces = res_face.shape[0]
    num_owned = num_faces // 4
    elements = res_inner.shape[0]
    num_coarse = coarse_inv.shape[1]
    counts = sharers[0]
    weights = jnp.where(counts > 0, 1.0 / jnp.maximum(counts, 1).astype(jnp.float32), 0.0)
    owner_onehot = (
        recv_index[0][None, :] == jnp.arange(num_owned, dtype=jnp.int32)[:, None]
    ).astype(jnp.bfloat16)

    def assemble(partials):
        received = send_out(partials)
        flattened = received.reshape(num_faces, -1)
        owner_sum = jnp.dot(owner_onehot, flattened, preferred_element_type=jnp.float32).astype(
            jnp.bfloat16
        )
        spread = jnp.einsum(
            "of,ok->fk", owner_onehot, owner_sum, preferred_element_type=jnp.float32
        ).astype(jnp.bfloat16)
        return send_back(spread.reshape(partials.shape))

    inner_w = jnp.einsum(
        "erb,ecb->erc", res_inner, inner_inv, preferred_element_type=jnp.float32
    ).astype(jnp.bfloat16)
    nearby = inner_w[face_elem[0]]
    condensed = res_face.astype(jnp.float32) - jnp.einsum(
        "lrb,lcb->lrc", nearby, face_coupling, preferred_element_type=jnp.float32
    )
    sent = (weights[:, None, None] * condensed).astype(jnp.bfloat16)
    gathered = assemble(sent)
    restricted = (weights[:, None, None] * gathered.astype(jnp.float32)).astype(jnp.bfloat16)
    local_coarse = jnp.einsum(
        "ljb,lrb->jr", coarse_basis, restricted, preferred_element_type=jnp.float32
    )
    coarse_onehot = (
        coarse_map[0][None, :] == jnp.arange(num_coarse, dtype=jnp.int32)[:, None]
    ).astype(jnp.float32)
    partial_rhs = jnp.dot(coarse_onehot, local_coarse, precision=lax.Precision.HIGHEST)
    share = sum_at_owner(partial_rhs, "grp", 0)
    rows_total = over_copies(share, "sub")
    column_term = lax.dot_general(
        coarse_inv, rows_total, (((0,), (0,)), ((), ())), precision=lax.Precision.HIGHEST
    )
    coarse_sol = over_copies(column_term, "grp")
    picked = jnp.einsum(
        "kj,kr->jr", coarse_onehot, coarse_sol, precision=lax.Precision.HIGHEST
    ).astype(jnp.bfloat16)
    coarse_part = jnp.einsum(
        "ljb,jr->lrb", coarse_basis, picked, preferred_element_type=jnp.float32
    )
    local_part = jnp.einsum(
        "lrb,lcb->lrc", restricted, face_inv, preferred_element_type=jnp.float32
    )
    weighted = (weights[:, None, None] * (coarse_part + local_part)).astype(jnp.bfloat16)
    face_out = assemble(weighted)
    contrib = jnp.einsum(
        "lrc,lcb->lrb", face_out, face_coupling, preferred_element_type=jnp.float32
    )
    elem_onehot = (face_elem[0][None, :] == jnp.arange(elements, dtype=jnp.int32)[:, None]).astype(
        jnp.float32
    )
    scattered = jnp.dot(
        elem_onehot, contrib.reshape(num_faces, -1), precision=lax.Precision.HIGHEST
    ).reshape(res_inner.shape)
    inner_rhs = (res_inner.astype(jnp.float32) - scattered).astype(jnp.bfloat16)
    inner_out = jnp.einsum(
        "erb,ecb->erc", inner_rhs, inner_inv, preferred_element_type=jnp.float32
    ).astype(jnp.bfloat16)
    return (inner_out, face_out)


def solution(mesh):
    return jax.shard_map(
        body,
        mesh=mesh,
        in_specs=(
            P(("sub", "grp"), None, None),
            P(("sub", "grp"), None, None),
            P(("sub", "grp"), None, None),
            P(("sub", "grp"), None, None),
            P(("sub", "grp"), None),
            P(("sub", "grp"), None, None),
            P(("sub", "grp"), None, None),
            P(("sub", "grp"), None),
            P("grp", None),
            P(("sub", "grp"), None),
            P(("sub", "grp"), None),
        ),
        out_specs=(P(("sub", "grp"), None, None), P(("sub", "grp"), None, None)),
        check_vma=False,
    )
```

profile of v0, /device:TPU:1, one launch (start us, length us, event | category | flops | bytes accessed | tf_op | source)
XLA Modules:
  0.0 211.0 jit_solution(2203128106772700261)
XLA Ops:
  2.1 2.6 %copy.55 = bf16[128,16,144]{2,1,0:T(8,128)(2,1)} copy(bf16[128,16,144]{0,2,1:T(8,128)(2,1)} %param.12) | data formatting | bytes 1179648 | tf_op args[1]
  4.7 13.3 %copy.56 = bf16[128,144,144]{2,1,0:T(8,128)(2,1)} copy(bf16[128,144,144]{0,2,1:T(8,128)(2,1)} %param.14) | data formatting | bytes 10616832 | tf_op args[3]
  18.1 3.6 %convolution_convert_fusion.5 = bf16[64,16,144]{2,1,0:T(8,128)(2,1)S(1)} fusion(bf16[64,16,144]{2,1,0:T(8,128)(2,1)S(1)} %copy-done.2, bf16[64,144,144]{2,1,0:T(8,128)(2,1)} %param.13), kind=kOutput, calls=%fused_computation.13 | convolution fusion | flops 42614784 | bytes 3244032 | tf_op jit(solution)/shard_map/erb,ecb->erc/dot_general | solution.py:70
  21.7 1.6 gather_fusion
  23.4 6.8 %multiply_convert_fusion.1 = bf16[128,16,144]{2,1,0:T(8,128)(2,1)S(1)} fusion(bf16[128,16,144]{2,1,0:T(8,128)(2,1)} %copy.55, bf16[128,16,144]{2,1,0:T(8,128)(2,1)} %gather_fusion, bf16[128,144,144]{2,1,0:T(8,128)(2,1)} %copy.56, f32[128]{0:T(128)S(1)} %fusion.17), kind=kOutput, calls=%fused_computation.10 | convolution fusion | flops 86114304 | bytes 7078400 | tf_op jit(solution)/shard_map/lrb,lcb->lrc/dot_general | solution.py:74
  30.1 30.6 %all_to_all.35 = bf16[128,16,144]{2,1,0:T(8,128)(2,1)S(1)} all-to-all(bf16[128,16,144]{2,1,0:T(8,128)(2,1)S(1)} %multiply_convert_fusion.1), channel_id=1, replica_groups=mesh['sub'=16,'grp'=8] {'sub','grp'}, dimensions={0} | all-to-all | bytes 1179648 | tf_op jit(solution)/shard_map/all_to_all | solution.py:29
  64.1 1.7 copy.59
  65.8 4.6 %all-to-all-start.1 = ((bf16[128,16,144]{2,1,0:T(8,128)(2,1)}), bf16[128,16,144]{2,1,0:T(8,128)(2,1)S(1)}, u32[]{:S(2)}, u32[]{:S(2)}) async-start(bf16[128,16,144]{2,1,0:T(8,128)(2,1)} %copy.59), calls=%async_computation.1 | async-start | bytes 2097152 | tf_op jit(solution)/shard_map/all_to_all | solution.py:33
  70.4 6.7 %copy.60 = bf16[128,64,144]{2,1,0:T(8,128)(2,1)} copy(bf16[128,64,144]{0,2,1:T(8,128)(2,1)} %param.17) | data formatting | bytes 4718592 | tf_op args[6]
  77.1 12.7 %all-to-all-done.1 = bf16[128,16,144]{2,1,0:T(8,128)(2,1)S(1)} async-done(((bf16[128,16,144]{2,1,0:T(8,128)(2,1)}), bf16[128,16,144]{2,1,0:T(8,128)(2,1)S(1)}, u32[]{:S(2)}, u32[]{:S(2)}) %all-to-all-start.1) | async-done | bytes 589856 | tf_op jit(solution)/shard_map/all_to_all | solution.py:33
  89.9 3.4 %convolution_bitcast_fusion.1 = f32[16,64]{1,0:T(8,128)S(1)} fusion(bf16[128,64,144]{2,1,0:T(8,128)(2,1)} %copy.60, bf16[128,16,144]{2,1,0:T(8,128)(2,1)S(1)} %all-to-all-done.1, f32[128]{0:T(128)S(1)} %fusion.17), kind=kOutput, calls=%fused_computation.16 | convolution fusion | flops 38633472 | bytes 2953728 | tf_op jit(solution)/shard_map/ljb,lrb->jr/dot_general | solution.py:80
  93.9 8.8 %all_to_all.36 = f32[8,256,16]{1,2,0:T(8,128)S(1)} all-to-all(f32[8,256,16]{1,2,0:T(8,128)S(1)} %bitcast.60), channel_id=1, replica_groups=mesh['sub'=16,'grp'=8] {'grp'}, dimensions={0} | all-to-all | bytes 262144 | tf_op jit(solution)/shard_map/all_to_all | solution.py:14
  102.8 10.0 %all_to_all.37 = f32[16,256,16]{1,2,0:T(8,128)S(1)} all-to-all(f32[16,256,16]{1,2,0:T(8,128)S(1)} %broadcast_in_dim.9), channel_id=1, replica_groups=mesh['sub'=16,'grp'=8] {'sub'}, dimensions={0} | all-to-all | bytes 524288 | tf_op jit(solution)/shard_map/all_to_all | solution.py:20
  115.0 5.8 %all-to-all-start.4 = ((f32[8,2048,16]{1,2,0:T(8,128)}), f32[8,2048,16]{1,2,0:T(8,128)S(1)}, u32[]{:S(2)}, u32[]{:S(2)}) async-start(f32[8,2048,16]{1,2,0:T(8,128)} %broadcast_in_dim.10), calls=%async_computation.4 | async-start | bytes 2097152 | tf_op jit(solution)/shard_map/all_to_all | solution.py:20
  120.8 13.3 %copy.64 = bf16[128,144,144]{2,1,0:T(8,128)(2,1)} copy(bf16[128,144,144]{0,2,1:T(8,128)(2,1)} %param.16) | data formatting | bytes 10616832 | tf_op args[5]
  134.0 1.9 all-to-all-done.4
  136.4 2.9 %fusion.18 = f32[16,128,144]{2,0,1:T(8,128)S(1)} fusion(bf16[64,16,1]{0,1,2:T(8,128)(2,1)S(1)} %fusion.4, bf16[128,64,144]{2,1,0:T(8,128)(2,1)} %copy.60), kind=kOutput, calls=%fused_computation.36 | convolution fusion | flops 37748736 | bytes 3540992 | tf_op jit(solution)/shard_map/ljb,jr->lrb/dot_general | solution.py:96
  139.2 6.3 %fusion.1 = bf16[128,16,144]{2,1,0:T(8,128)(2,1)S(1)} fusion(f32[16,128,144]{2,0,1:T(8,128)S(1)} %fusion.18, bf16[128,144,144]{2,1,0:T(8,128)(2,1)} %copy.64, f32[128]{0:T(128)S(1)} %fusion.17, bf16[128,16,144]{2,1,0:T(8,128)(2,1)S(1)} %all-to-all-done.1), kind=kOutput, calls=%fused_computation.8 | convolution fusion | flops 86704128 | bytes 7668224 | tf_op jit(solution)/shard_map/lrb,lcb->lrc/dot_general | solution.py:99
  145.5 23.7 %all_to_all.38 = bf16[128,16,144]{2,1,0:T(8,128)(2,1)S(1)} all-to-all(bf16[128,16,144]{2,1,0:T(8,128)(2,1)S(1)} %fusion.1), channel_id=1, replica_groups=mesh['sub'=16,'grp'=8] {'sub','grp'}, dimensions={0} | all-to-all | bytes 1179648 | tf_op jit(solution)/shard_map/all_to_all | solution.py:29
  171.8 23.6 %all_to_all.39 = bf16[128,16,144]{2,1,0:T(8,128)(2,1)S(1)} all-to-all(bf16[128,16,144]{2,1,0:T(8,128)(2,1)S(1)} %copy.67), channel_id=1, replica_groups=mesh['sub'=16,'grp'=8] {'sub','grp'}, dimensions={0} | all-to-all | bytes 1179648 | tf_op jit(solution)/shard_map/all_to_all | solution.py:33
  195.4 5.0 %fusion.19 = f32[128,16,144]{2,1,0:T(8,128)S(1)} fusion(bf16[128,16,144]{2,1,0:T(8,128)(2,1)S(1)} %all_to_all.39, bf16[128,144,144]{2,1,0:T(8,128)(2,1)} %copy.56), kind=kOutput, calls=%fused_computation.37 | convolution fusion | flops 84934656 | bytes 7077888 | tf_op jit(solution)/shard_map/lrc,lcb->lrb/dot_general | solution.py:104
  200.4 1.7 copy.69
  202.1 2.7 %fusion.2 = bf16[64,16,144]{2,0,1:T(8,128)(2,1)S(1)} fusion(f32[128,16,144]{0,2,1:T(8,128)} %copy.69, bf16[64,16,144]{2,1,0:T(8,128)(2,1)} %param.11, s32[128]{0:T(128)S(1)} %bitcast.64), kind=kOutput, calls=%fused_computation.14 | convolution fusion | flops 226942976 | bytes 1769984 | tf_op jit(solution)/shard_map/dot_general | solution.py:110
  204.8 4.6 %convolution_convert_fusion.4 = bf16[64,16,144]{2,1,0:T(8,128)(2,1)} fusion(bf16[64,144,144]{2,1,0:T(8,128)(2,1)} %param.13, bf16[64,16,144]{2,0,1:T(8,128)(2,1)S(1)} %fusion.2), kind=kOutput, calls=%fused_computation.12 | convolution fusion | flops 42614784 | bytes 3244032 | tf_op jit(solution)/shard_map/erb,ecb->erc/dot_general | solution.py:114
  (32 shorter events, 12.5 us)
Async XLA Ops:
  0.6 112.2 %copy-start = (f32[256,2048]{1,0:T(8,128)S(1)}, f32[256,2048]{1,0:T(8,128)}, u32[]{:S(2)}) copy-start(f32[256,2048]{1,0:T(8,128)} %param.19) | copy-start | bytes 6291460
  4.7 13.3 %copy-start.2 = (bf16[64,16,144]{2,1,0:T(8,128)(2,1)S(1)}, bf16[64,16,144]{2,1,0:T(8,128)(2,1)}, u32[]{:S(2)}) copy-start(bf16[64,16,144]{2,1,0:T(8,128)(2,1)} %param.11) | copy-start | bytes 884740
  30.1 32.2 %copy-start.3 = (s32[1,128]{1,0:T(1,128)S(1)}, s32[1,128]{1,0:T(1,128)}, u32[]{:S(2)}) copy-start(s32[1,128]{1,0:T(1,128)} %param.20) | copy-start | bytes 1540
  65.8 24.0 %all-to-all-start.1 = ((bf16[128,16,144]{2,1,0:T(8,128)(2,1)}), bf16[128,16,144]{2,1,0:T(8,128)(2,1)S(1)}, u32[]{:S(2)}, u32[]{:S(2)}) async-start(bf16[128,16,144]{2,1,0:T(8,128)(2,1)} %copy.59), calls=%async_computation.1 | async-start | bytes 2097152 | tf_op jit(solution)/shard_map/all_to_all | solution.py:33
  77.1 16.2 %copy-start.5 = (s32[1,64]{1,0:T(1,128)S(1)}, s32[1,64]{1,0:T(1,128)}, u32[]{:S(2)}) copy-start(s32[1,64]{1,0:T(1,128)} %param.18) | copy-start | bytes 772
  115.0 20.9 %all-to-all-start.4 = ((f32[8,2048,16]{1,2,0:T(8,128)}), f32[8,2048,16]{1,2,0:T(8,128)S(1)}, u32[]{:S(2)}, u32[]{:S(2)}) async-start(f32[8,2048,16]{1,2,0:T(8,128)} %broadcast_in_dim.10), calls=%async_computation.4 | async-start | bytes 2097152 | tf_op jit(solution)/shard_map/all_to_all | solution.py:20
  200.4 1.7 copy-start.4
  204.8 6.2 %copy-start.1 = (f32[256,2048]{1,0:T(8,128)S(1)}, f32[256,2048]{1,0:T(8,128)}, u32[]{:S(2)}) copy-start(f32[256,2048]{1,0:T(8,128)} %param.19) | copy-start | bytes 6291460
where the time goes:
time: 212 us; the launch traced here: 211 us
  blocking collectives  96.6 us (46%)
  local copies, waits for them, and re-layouts  47.7 us (22%)
  matrix products  39.5 us (19%)
  waiting for transfers between devices  14.6 us (7%)
  starting transfers between devices  10.3 us (5%)
    all_to_all x2, blocking collectives, send_out(): lax.all_to_all(partials, ('sub', 'grp'), split_axis=0, concat_axis=0, til...  54.2 us
    unnamed x17, local copies, waits for them, and re-layouts  37.5 us
    all_to_all x1, blocking collectives, send_back(): lax.all_to_all(spread, ('sub', 'grp'), split_axis=0, concat_axis=0, tiled...  23.6 us
    all_to_all x1, waiting for transfers between devices, send_back(): lax.all_to_all(spread, ('sub', 'grp'), split_axis=0, concat_axis=0, tiled...  12.7 us
    all_to_all x1, blocking collectives, copy_for_each(): lax.all_to_all(jnp.broadcast_to(x[None], (size, *x.shape)), axis, 0, 0, t...  9.98 us
    all_to_all x1, blocking collectives, sum_at_owner(): blocks = lax.all_to_all(cut_along(x, dim, size), axis, 0, 0, tiled=True)  8.82 us
    dot_general x1, matrix products, body(): jnp.einsum('lrb,lcb->lrc', nearby, face_coupling, preferred_element_type=...  6.75 us
    dot_general x1, matrix products, body(): jnp.einsum('lrb,lcb->lrc', restricted, face_inv, preferred_element_type=j...  6.27 us
  transfers between devices with their start and end apart: 2, of which 2 were waited for; matrix products, arithmetic and copies ran while one was open for 9% of the time, Pallas kernels for 0%

commit v1 on v0

--- a/solution.py
+++ b/solution.py
@@ -1,7 +1,93 @@
 import jax
 import jax.numpy as jnp
 from jax import lax
+from jax.experimental import pallas as pl
+from jax.experimental.pallas import tpu as pltpu
 from jax.sharding import PartitionSpec as P
+
+MESH = pl.DeviceIdType.MESH
+N = 128
+ROWS = 18
+PITCH = 24
+
+
+def place(t):
+    return (t // 8, t % 8)
+
+
+def assemble_kernel(x_ref, row_ref, col_ref, o_ref, recv, wide, wide2, back, ssem, rsem, lsem, ssem2, rsem2, lsem2):
+    me = lax.axis_index("sub") * 8 + lax.axis_index("grp")
+    barrier = pltpu.get_barrier_semaphore()
+
+    def greet(i, c):
+        pl.semaphore_signal(barrier, inc=1, device_id=place(lax.rem(me + i, N)), device_id_type=MESH)
+        return c
+
+    lax.fori_loop(1, N, greet, 0)
+    pl.semaphore_wait(barrier, N - 1)
+
+    def remote(src, dst, t, s, r):
+        return pltpu.make_async_remote_copy(
+            src_ref=src, dst_ref=dst, send_sem=s, recv_sem=r, device_id=place(t), device_id_type=MESH
+        )
+
+    def send(i, c):
+        t = lax.rem(me + i, N)
+        remote(x_ref.at[t], recv.at[me], t, ssem, rsem).start()
+        return c
+
+    own = pltpu.make_async_copy(x_ref.at[me], recv.at[me], lsem)
+    own.start()
+    lax.fori_loop(1, N, send, 0)
+    own.wait()
+    rest = pl.ds(0, N - 1)
+    remote(x_ref.at[rest], recv.at[rest], 0, ssem, rsem).wait()
+
+    def widen(s, c):
+        wide[pl.ds(pl.multiple_of(s * PITCH, 8), ROWS)] = recv[s].astype(jnp.float32)
+        return c
+
+    lax.fori_loop(0, N, widen, 0)
+    same = jnp.where((row_ref[...] == col_ref[...]) & (row_ref[...] < 32), 1.0, 0.0).astype(jnp.bfloat16)
+    for k in range(ROWS):
+        part = wide[pl.ds(k, N, stride=PITCH), :].astype(jnp.bfloat16)
+        wide2[pl.ds(k, N, stride=PITCH), :] = jnp.dot(same, part, preferred_element_type=jnp.float32)
+
+    def give(i, c):
+        t = lax.rem(me + i, N)
+        back[t] = wide2[pl.ds(pl.multiple_of(t * PITCH, 8), ROWS)].astype(jnp.bfloat16)
+        remote(back.at[t], o_ref.at[me], t, ssem2, rsem2).start()
+        return c
+
+    back[me] = wide2[pl.ds(pl.multiple_of(me * PITCH, 8), ROWS)].astype(jnp.bfloat16)
+    own = pltpu.make_async_copy(back.at[me], o_ref.at[me], lsem2)
+    own.start()
+    lax.fori_loop(1, N, give, 0)
+    own.wait()
+    remote(back.at[rest], o_ref.at[rest], 0, ssem2, rsem2).wait()
+
+
+def assemble(x, index):
+    vm = pl.BlockSpec(memory_space=pltpu.VMEM)
+    packed = jax.ShapeDtypeStruct((N, ROWS, 128), jnp.bfloat16)
+    out = pl.pallas_call(
+        assemble_kernel,
+        out_shape=packed,
+        in_specs=[vm] * 3,
+        out_specs=vm,
+        scratch_shapes=[
+            pltpu.VMEM((N, ROWS, 128), jnp.bfloat16),
+            pltpu.VMEM((N * PITCH, 128), jnp.float32),
+            pltpu.VMEM((N * PITCH, 128), jnp.float32),
+            pltpu.VMEM((N, ROWS, 128), jnp.bfloat16),
+        ]
+        + [pltpu.SemaphoreType.DMA] * 6,
+        name="assemble",
+        compiler_params=pltpu.CompilerParams(
+            collective_id=0, has_side_effects=True, vmem_limit_bytes=32 << 20
+        ),
+    )(x.reshape(N, ROWS, 128), index.reshape(1, N), index.reshape(N, 1))
+    return out.reshape(x.shape)
 
 
 def cut_along(x, dim, size):
@@ -23,14 +109,6 @@
 def over_copies(x, axis):
     everything = copy_for_each(x, axis)
     return jnp.sum(everything, axis=0)
-
-
-def send_out(partials):
-    return lax.all_to_all(partials, ("sub", "grp"), split_axis=0, concat_axis=0, tiled=True)
-
-
-def send_back(spread):
-    return lax.all_to_all(spread, ("sub", "grp"), split_axis=0, concat_axis=0, tiled=True)
 
 
 def body(
@@ -47,35 +125,24 @@
     sharers,
 ):
     num_faces = res_face.shape[0]
-    num_owned = num_faces // 4
     elements = res_inner.shape[0]
     num_coarse = coarse_inv.shape[1]
     counts = sharers[0]
     weights = jnp.where(counts > 0, 1.0 / jnp.maximum(counts, 1).astype(jnp.float32), 0.0)
-    owner_onehot = (
-        recv_index[0][None, :] == jnp.arange(num_owned, dtype=jnp.int32)[:, None]
-    ).astype(jnp.bfloat16)
-
-    def assemble(partials):
-        received = send_out(partials)
-        flattened = received.reshape(num_faces, -1)
-        owner_sum = jnp.dot(owner_onehot, flattened, preferred_element_type=jnp.float32).astype(
-            jnp.bfloat16
-        )
-        spread = jnp.einsum(
-            "of,ok->fk", owner_onehot, owner_sum, preferred_element_type=jnp.float32
-        ).astype(jnp.bfloat16)
-        return send_back(spread.reshape(partials.shape))
-
     inner_w = jnp.einsum(
         "erb,ecb->erc", res_inner, inner_inv, preferred_element_type=jnp.float32
     ).astype(jnp.bfloat16)
-    nearby = inner_w[face_elem[0]]
+    pick_elem = (face_elem[0][:, None] == jnp.arange(elements, dtype=jnp.int32)[None, :]).astype(
+        jnp.bfloat16
+    )
+    nearby = jnp.dot(
+        pick_elem, inner_w.reshape(elements, -1), preferred_element_type=jnp.float32
+    ).astype(jnp.bfloat16).reshape(res_face.shape)
     condensed = res_face.astype(jnp.float32) - jnp.einsum(
         "lrb,lcb->lrc", nearby, face_coupling, preferred_element_type=jnp.float32
     )
     sent = (weights[:, None, None] * condensed).astype(jnp.bfloat16)
-    gathered = assemble(sent)
+    gathered = assemble(sent, recv_index[0])
     restricted = (weights[:, None, None] * gathered.astype(jnp.float32)).astype(jnp.bfloat16)
     local_coarse = jnp.einsum(
         "ljb,lrb->jr", coarse_basis, restricted, preferred_element_type=jnp.float32
@@ -100,7 +167,7 @@
         "lrb,lcb->lrc", restricted, face_inv, preferred_element_type=jnp.float32
     )
     weighted = (weights[:, None, None] * (coarse_part + local_part)).astype(jnp.bfloat16)
-    face_out = assemble(weighted)
+    face_out = assemble(weighted, recv_index[0])
     contrib = jnp.einsum(
         "lrc,lcb->lrb", face_out, face_coupling, preferred_element_type=jnp.float32
     )

time: 212 us -> 197 us (0.929)
  blocking collectives: 96.6 us -> 22 us
  Pallas kernels: 0 us -> 72.8 us
  waiting for transfers between devices: 14.6 us -> 1.86 us
  local copies, waits for them, and re-layouts: 47.7 us -> 52.3 us
  starting transfers between devices: 10.3 us -> 5.75 us
    all_to_all x3 -> x0, blocking collectives: 77.8 us -> none  [the longest x2 54.2 us: send_out(): lax.all_to_all(partials, ('sub', 'grp'), split_axis=0, concat_axis=0, til...]
    pallas_call x0 -> x2, Pallas kernels: none -> 72.8 us  [assemble(): pl.pallas_call(assemble_kernel, out_shape=packed, in_specs=[vm] * 3, out_...]
    all_to_all x1 -> x0, waiting for transfers between devices: 12.7 us -> none  [send_back(): lax.all_to_all(spread, ('sub', 'grp'), split_axis=0, concat_axis=0, tiled...]
    convert_element_type x2 -> x5, local copies, waits for them, and re-layouts: 0.6 us -> 7.38 us  [the longest x2 3.48 us: body(): gathered.astype(jnp.float32)]
    all_to_all x1 -> x0, starting transfers between devices: 4.59 us -> none  [send_back(): lax.all_to_all(spread, ('sub', 'grp'), split_axis=0, concat_axis=0, tiled...]
    all_to_all x1, blocking collectives: 9.98 us -> 13 us  [copy_for_each(): lax.all_to_all(jnp.broadcast_to(x[None], (size, *x.shape)), axis, 0, 0, t...]
    all_to_all x2 -> x0, local copies, waits for them, and re-layouts: 2.53 us -> none  [send_out(): lax.all_to_all(partials, ('sub', 'grp'), split_axis=0, concat_axis=0, til...]
    unnamed x17 -> x20, local copies, waits for them, and re-layouts: 37.5 us -> 37.5 us
  transfers between devices with their start and end apart: 2 -> 1, of which waited for: 2 -> 1; matrix products, arithmetic and copies ran while one was open for 9% -> 7% of each run, Pallas kernels for 0% -> 0%
where the time goes in v1:
time: 197 us; the launch traced here: 196 us
  Pallas kernels  72.8 us (37%)
  local copies, waits for them, and re-layouts  52.3 us (27%)
  matrix products  39.2 us (20%)
  blocking collectives  22 us (11%)
  starting transfers between devices  5.75 us (3%)
    pallas_call x2, Pallas kernels, assemble(): pl.pallas_call(assemble_kernel, out_shape=packed, in_specs=[vm] * 3, out_...  72.8 us
    unnamed x20, local copies, waits for them, and re-layouts  37.5 us
    all_to_all x1, blocking collectives, copy_for_each(): lax.all_to_all(jnp.broadcast_to(x[None], (size, *x.shape)), axis, 0, 0, t...  13 us
    all_to_all x1, blocking collectives, sum_at_owner(): blocks = lax.all_to_all(cut_along(x, dim, size), axis, 0, 0, tiled=True)  9 us
    dot_general x1, matrix products, body(): jnp.einsum('lrb,lcb->lrc', nearby, face_coupling, preferred_element_type=...  7.43 us
    dot_general x1, matrix products, body(): jnp.einsum('lrb,lcb->lrc', restricted, face_inv, preferred_element_type=j...  6.34 us
    all_to_all x1, starting transfers between devices, copy_for_each(): lax.all_to_all(jnp.broadcast_to(x[None], (size, *x.shape)), axis, 0, 0, t...  5.75 us
    dot_general x1, matrix products, body(): jnp.einsum('lrc,lcb->lrb', face_out, face_coupling, preferred_element_typ...  5.01 us
  transfers between devices with their start and end apart: 1, of which 1 were waited for; matrix products, arithmetic and copies ran while one was open for 7% of the time, Pallas kernels for 0%

profile of v1, /device:TPU:1, one launch (start us, length us, event | category | flops | bytes accessed | tf_op | source)
XLA Modules:
  0.0 195.6 jit_solution(7006787653753706719)
XLA Ops:
  2.2 3.8 %convolution_convert_fusion.2 = bf16[64,16,144]{2,1,0:T(8,128)(2,1)S(1)} fusion(bf16[64,16,144]{2,1,0:T(8,128)(2,1)} %param.11, bf16[64,144,144]{2,1,0:T(8,128)(2,1)} %param.13), kind=kOutput, calls=%fused_computation.9 | convolution fusion | flops 42614784 | bytes 3244032 | tf_op jit(solution)/shard_map/erb,ecb->erc/dot_general | solution.py:132
  8.1 1.8 copy.92
  9.9 2.6 %copy.90 = bf16[128,16,144]{2,1,0:T(8,128)(2,1)} copy(bf16[128,16,144]{0,2,1:T(8,128)(2,1)} %param.12) | data formatting | bytes 1179648 | tf_op args[1]
  12.5 6.6 %copy.99 = bf16[128,64,144]{2,1,0:T(8,128)(2,1)} copy(bf16[128,64,144]{0,2,1:T(8,128)(2,1)} %param.17) | data formatting | bytes 4718592 | tf_op args[6]
  19.2 13.3 %copy.93 = bf16[128,144,144]{2,1,0:T(8,128)(2,1)} copy(bf16[128,144,144]{0,2,1:T(8,128)(2,1)} %param.14) | data formatting | bytes 10616832 | tf_op args[3]
  32.4 7.4 %multiply_convert_fusion.1 = bf16[128,16,144]{2,1,0:T(8,128)(2,1)} fusion(bf16[128,16,144]{2,1,0:T(8,128)(2,1)} %copy.90, bf16[128,16,144]{2,1,0:T(8,128)(2,1)S(1)} %copy.92, bf16[128,144,144]{2,1,0:T(8,128)(2,1)} %copy.93, f32[128]{0:T(128)S(1)} %fusion.13), kind=kOutput, calls=%fused_computation.6 | convolution fusion | flops 86114304 | bytes 7078400 | tf_op jit(solution)/shard_map/lrb,lcb->lrc/dot_general | solution.py:141
  39.9 1.9 copy.94
  42.2 39.2 %assemble.2 = bf16[128,18,128]{2,1,0:T(8,128)(2,1)S(1)} custom-call(bf16[128,18,128]{2,1,0:T(8,128)(2,1)S(1)} %copy.95.x_ref, s32[1,128]{1,0:T(1,128)S(1)} %copy-done.3, s32[128,1]{1,0:T(8,128)S(1)} %copy.96.col_ref), custom_call_target="tpu_custom_call" | custom-call | tf_op jit(solution)/shard_map/assemble/pallas_call | solution.py:73
  82.3 1.5 copy.97
  83.8 1.9 copy.98
  85.8 4.1 %convolution_bitcast_fusion.1 = f32[16,64]{1,0:T(8,128)S(1)} fusion(bf16[128,64,144]{2,1,0:T(8,128)(2,1)} %copy.99, f32[128,16,144]{2,1,0:T(8,128)} %copy.98, f32[128]{0:T(128)S(1)} %fusion.13), kind=kOutput, calls=%fused_computation.12 | convolution fusion | flops 38338560 | bytes 3543552 | tf_op jit(solution)/shard_map/ljb,lrb->jr/dot_general | solution.py:147
  90.5 9.0 %all_to_all.15 = f32[8,256,16]{1,2,0:T(8,128)S(1)} all-to-all(f32[8,256,16]{1,2,0:T(8,128)S(1)} %bitcast.59), channel_id=1, replica_groups=mesh['sub'=16,'grp'=8] {'grp'}, dimensions={0} | all-to-all | bytes 262144 | tf_op jit(solution)/shard_map/all_to_all | solution.py:100
  99.5 13.0 %all_to_all.16 = f32[16,256,16]{1,2,0:T(8,128)S(1)} all-to-all(f32[16,256,16]{1,2,0:T(8,128)S(1)} %broadcast_in_dim.9), channel_id=1, replica_groups=mesh['sub'=16,'grp'=8] {'sub'}, dimensions={0} | all-to-all | bytes 524288 | tf_op jit(solution)/shard_map/all_to_all | solution.py:106
  112.5 1.1 convolution_bitcast_fusion
  113.6 1.2 broadcast_in_dim.10
  114.8 5.8 %all-to-all-start.2 = ((f32[8,2048,16]{1,2,0:T(8,128)}), f32[8,2048,16]{1,2,0:T(8,128)S(1)}, u32[]{:S(2)}, u32[]{:S(2)}) async-start(f32[8,2048,16]{1,2,0:T(8,128)} %broadcast_in_dim.10), calls=%async_computation.2 | async-start | bytes 2097152 | tf_op jit(solution)/shard_map/all_to_all | solution.py:106
  120.5 13.3 %copy.103 = bf16[128,144,144]{2,1,0:T(8,128)(2,1)} copy(bf16[128,144,144]{0,2,1:T(8,128)(2,1)} %param.16) | data formatting | bytes 10616832 | tf_op args[5]
  133.8 1.9 all-to-all-done.2
  136.2 3.0 %fusion.14 = f32[16,128,144]{2,0,1:T(8,128)S(1)} fusion(bf16[64,16,1]{0,1,2:T(8,128)(2,1)S(1)} %fusion.4, bf16[128,64,144]{2,1,0:T(8,128)(2,1)} %copy.99), kind=kOutput, calls=%fused_computation.28 | convolution fusion | flops 37748736 | bytes 3540992 | tf_op jit(solution)/shard_map/ljb,jr->lrb/dot_general | solution.py:163
  139.2 6.3 %fusion.1 = bf16[128,16,144]{2,1,0:T(8,128)(2,1)S(1)} fusion(f32[16,128,144]{2,0,1:T(8,128)S(1)} %fusion.14, bf16[128,144,144]{2,1,0:T(8,128)(2,1)} %copy.103, f32[128]{0:T(128)S(1)} %fusion.13, f32[128,16,144]{2,1,0:T(8,128)S(1)} %copy-done.4), kind=kOutput, calls=%fused_computation.4 | convolution fusion | flops 86409216 | bytes 8258048 | tf_op jit(solution)/shard_map/lrb,lcb->lrc/dot_general | solution.py:166
  146.9 33.7 %assemble.3 = bf16[128,18,128]{2,1,0:T(8,128)(2,1)S(1)} custom-call(bf16[128,18,128]{2,1,0:T(8,128)(2,1)S(1)} %copy.105.x_ref, s32[1,128]{1,0:T(1,128)S(1)} %copy-done.3, s32[128,1]{1,0:T(8,128)S(1)} %copy.96.col_ref), custom_call_target="tpu_custom_call" | custom-call | tf_op jit(solution)/shard_map/assemble/pallas_call | solution.py:73
  182.7 5.0 %fusion.15 = f32[128,16,144]{2,1,0:T(8,128)S(1)} fusion(bf16[128,16,144]{2,1,0:T(8,128)(2,1)S(1)} %copy.108, bf16[128,144,144]{2,1,0:T(8,128)(2,1)} %copy.93), kind=kOutput, calls=%fused_computation.29 | convolution fusion | flops 84934656 | bytes 7077888 | tf_op jit(solution)/shard_map/lrc,lcb->lrb/dot_general | solution.py:171
  188.7 2.5 %fusion.2 = bf16[64,16,144]{2,0,1:T(8,128)(2,1)S(1)} fusion(f32[128,16,144]{0,2,1:T(8,128)S(1)} %copy.110, bf16[64,16,144]{2,1,0:T(8,128)(2,1)} %param.11, s32[128]{0:T(128)S(1)} %bitcast.62), kind=kOutput, calls=%fused_computation.10 | convolution fusion | flops 226942976 | bytes 1769984 | tf_op jit(solution)/shard_map/dot_general | solution.py:177
  191.2 4.5 %convolution_convert_fusion.1 = bf16[64,16,144]{2,1,0:T(8,128)(2,1)} fusion(bf16[64,144,144]{2,1,0:T(8,128)(2,1)} %param.13, bf16[64,16,144]{2,0,1:T(8,128)(2,1)S(1)} %fusion.2), kind=kOutput, calls=%fused_computation.8 | convolution fusion | flops 42614784 | bytes 3244032 | tf_op jit(solution)/shard_map/erb,ecb->erc/dot_general | solution.py:181
  (34 shorter events, 10.6 us)
Async XLA Ops:
  0.6 111.9 %copy-start = (f32[256,2048]{1,0:T(8,128)S(1)}, f32[256,2048]{1,0:T(8,128)}, u32[]{:S(2)}) copy-start(f32[256,2048]{1,0:T(8,128)} %param.19) | copy-start | bytes 6291460
  2.2 4.5 %copy-start.6 = (s32[1,128]{1,0:T(1,128)S(1)}, s32[1,128]{1,0:T(1,128)}, u32[]{:S(2)}) copy-start(s32[1,128]{1,0:T(1,128)} %param.15) | copy-start | bytes 1540
  39.9 2.3 %copy-start.3 = (s32[1,128]{1,0:T(1,128)S(1)}, s32[1,128]{1,0:T(1,128)}, u32[]{:S(2)}) copy-start(s32[1,128]{1,0:T(1,128)} %row_ref.3) | copy-start | bytes 1540
  81.4 0.9 copy-start.2
  85.8 4.1 %copy-start.7 = (s32[1,64]{1,0:T(1,128)S(1)}, s32[1,64]{1,0:T(1,128)}, u32[]{:S(2)}) copy-start(s32[1,64]{1,0:T(1,128)} %param.18) | copy-start | bytes 772
  114.8 20.9 %all-to-all-start.2 = ((f32[8,2048,16]{1,2,0:T(8,128)}), f32[8,2048,16]{1,2,0:T(8,128)S(1)}, u32[]{:S(2)}, u32[]{:S(2)}) async-start(f32[8,2048,16]{1,2,0:T(8,128)} %broadcast_in_dim.10), calls=%async_computation.2 | async-start | bytes 2097152 | tf_op jit(solution)/shard_map/all_to_all | solution.py:106
  136.1 3.0 %copy-start.4 = (f32[128,16,144]{2,1,0:T(8,128)S(1)}, f32[128,16,144]{2,1,0:T(8,128)}, u32[]{:S(2)}) copy-start(f32[128,16,144]{2,1,0:T(8,128)} %copy.98) | copy-start | bytes 3538948
  181.0 0.8 copy-start.5
  188.6 7.0 %copy-start.1 = (f32[256,2048]{1,0:T(8,128)S(1)}, f32[256,2048]{1,0:T(8,128)}, u32[]{:S(2)}) copy-start(f32[256,2048]{1,0:T(8,128)} %param.19) | copy-start | bytes 6291460

commit v2 on v0

v2 whole, which is shorter than its diff:
```python
import jax
import jax.numpy as jnp
from jax import lax
from jax.experimental import pallas as pl
from jax.experimental.pallas import tpu as pltpu
from jax.sharding import PartitionSpec as P

MESH = pl.DeviceIdType.MESH
N = 128
E = 64
R = 16
B = 144
NC = 64
NCG = 2048
GRP = 8
SUB = 16
SHARE = NCG // GRP
ROWS = 18
PITCH = 24
BF = jnp.bfloat16
F32 = jnp.float32


def place(t):
    return (t // GRP, t % GRP)


def remote(src, dst, device, s, r):
    return pltpu.make_async_remote_copy(
        src_ref=src, dst_ref=dst, send_sem=s, recv_sem=r, device_id=device, device_id_type=MESH
    )


def own_group():
    row = lax.broadcasted_iota(jnp.int32, (R, 128), 0)
    lane = lax.broadcasted_iota(jnp.int32, (R, 128), 1)
    return (row % 8) == (lane // 16)


def pack(out, t, value):
    out[t, 0:R, :] = value[:, 0:128].astype(BF)
    tail = jnp.where(own_group(), jnp.concatenate([value[:, 128:B]] * 8, axis=1), 0.0)
    out[t, R:ROWS, :] = jnp.sum(tail.reshape(2, 8, 128), axis=1).astype(BF)


def unpack(ref, t):
    tail = ref[t, R:ROWS, :].astype(F32)
    tail = jnp.broadcast_to(tail[:, None, :], (2, 8, 128)).reshape(R, 128)
    tail = jnp.where(own_group(), tail, 0.0)
    for shift in (64, 32, 16):
        tail = tail + pltpu.roll(tail, shift, 1)
    return jnp.concatenate([ref[t, 0:R, :].astype(F32), tail[:, 0:16]], axis=1)


def pieces(x):
    high = x.astype(BF)
    rest = x - high.astype(F32)
    mid = rest.astype(BF)
    low = (rest - mid.astype(F32)).astype(BF)
    return jnp.concatenate([high, mid, low], axis=0)


def gather3(x):
    return x[0:R] + x[R : 2 * R] + x[2 * R : 3 * R]


def rows_times(a, b):
    return lax.dot_general(a, b, (((1,), (1,)), ((), ())), preferred_element_type=F32)


def main_kernel(
    res_inner_h, res_face_h, inner_inv_h, coupling_h, face_inv_h, basis_h, coarse_inv_h,
    map_block, map_col, index_row, index_col, elem, weight,
    result, coupling_out,
    res_inner, inner_inv, inner_w, res_face, face_rows, stage, coupling, face_inv, basis_stage, basis,
    coarse_inv, coarse_high, coarse_low, pick, own_pick, maps,
    sent, received, wide, wide2, back, gathered, restricted, local,
    part, part_in, share, share_in, chosen, chosen_in,
    load_sems, send_sems, recv_sems, own_sems,
):
    sub = lax.axis_index("sub")
    grp = lax.axis_index("grp")
    me = sub * GRP + grp
    barrier = pltpu.get_barrier_semaphore()

    def load(src, dst, k):
        return pltpu.make_async_copy(src, dst, load_sems.at[k])

    load(res_inner_h, res_inner, 0).start()
    load(inner_inv_h, inner_inv, 1).start()
    load(coupling_h, stage, 2).start()
    load(res_face_h, res_face, 3).start()
    load(basis_h, basis_stage, 4).start()
    load(coarse_inv_h, coarse_inv, 5).start()

    def greet(i):
        pl.semaphore_signal(barrier, inc=1, device_id=place(lax.rem(me + i, N)), device_id_type=MESH)

    def inner(e, c):
        inner_w[e] = rows_times(res_inner[e], inner_inv[e]).astype(BF)
        return c

    def inner_greet(e, c):
        greet(2 * e)
        greet(2 * e + 1)
        return inner(e, c)

    load(res_inner_h, res_inner, 0).wait()
    load(inner_inv_h, inner_inv, 1).wait()
    greet(1)
    inner(0, 0)
    lax.fori_loop(1, E, inner_greet, 0, unroll=3)

    def turn(src, dst, q):
        part_rows = src[pl.ds(pl.multiple_of(q * 16, 16), 16)]
        part_rows = jnp.swapaxes(jnp.swapaxes(part_rows, 1, 2), 0, 1)
        dst[:, pl.ds(pl.multiple_of(q * 16, 16), 16), :] = part_rows

    def turns(src, dst, first, last):
        def one(q, c):
            turn(src, dst, q)
            return c

        lax.fori_loop(first, last, one, 0)

    load(res_face_h, res_face, 3).wait()
    turns(res_face, face_rows, 0, 1)
    load(coupling_h, stage, 2).wait()
    turns(stage, coupling, 0, 9)
    load(face_inv_h, stage, 6).start()
    save = load(coupling, coupling_out, 7)
    save.start()

    pl.semaphore_wait(barrier, N - 1)

    def map_copy(i):
        return remote(map_block, maps.at[grp], (sub, lax.rem(grp + i, GRP)), send_sems.at[0], recv_sems.at[0])

    def each(first, last, f, unroll=1):
        def one(i, c):
            f(i)
            return c

        lax.fori_loop(first, last, one, 0, unroll=unroll)

    own_map = pltpu.make_async_copy(map_block, maps.at[grp], own_sems.at[0])
    own_map.start()
    each(1, GRP, lambda i: map_copy(i).start())

    def exchange(source, target, k, fill, unroll):
        fill(me)
        own = pltpu.make_async_copy(source.at[me], target.at[me], own_sems.at[k])
        own.start()

        def one(i):
            t = lax.rem(me + i, N)
            fill(t)
            remote(source.at[t], target.at[me], place(t), send_sems.at[k], recv_sems.at[k]).start()

        each(1, N, one, unroll)
        return own

    def arrive(source, target, k, own):
        own.wait()
        rest = pl.ds(0, N - 1)
        remote(source.at[rest], target.at[rest], (sub, grp), send_sems.at[k], recv_sems.at[k]).wait()

    def condense(t):
        product = rows_times(inner_w[elem[t]], coupling[t])
        pack(sent.at[0], t, weight[t] * (face_rows[t].astype(F32) - product))

    own = exchange(sent.at[0], received.at[0], 1, condense, 4)
    load(face_inv_h, stage, 6).wait()
    turns(stage, face_inv, 0, 4)
    arrive(sent.at[0], received.at[0], 1, own)

    same = jnp.where((index_row[...] == index_col[...]) & (index_row[...] < 32), 1.0, 0.0).astype(BF)

    def owner_sum(source):
        def widen(s):
            wide[pl.ds(pl.multiple_of(s * PITCH, 8), ROWS)] = source[s].astype(F32)

        each(0, N, widen, 4)
        for k in range(ROWS):
            rows = wide[pl.ds(k, N, stride=PITCH), :].astype(BF)
            wide2[pl.ds(k, N, stride=PITCH), :] = jnp.dot(same, rows, preferred_element_type=F32)

    def narrow(target):
        def one(t):
            target[t] = wide2[pl.ds(pl.multiple_of(t * PITCH, 8), ROWS)].astype(BF)

        return one

    owner_sum(received.at[0])
    own = exchange(back.at[0], gathered, 2, narrow(back.at[0]), 4)

    turns(stage, face_inv, 4, 9)
    load(basis_h, basis_stage, 4).wait()
    turns(basis_stage, basis, 0, 4)
    load(coarse_inv_h, coarse_inv, 5).wait()

    def split(q):
        rows = pl.ds(pl.multiple_of(q * 16, 16), 16)
        high = coarse_inv[rows, :].astype(BF)
        coarse_high[rows, :] = high
        coarse_low[rows, :] = (coarse_inv[rows, :] - high.astype(F32)).astype(BF)

    each(0, SHARE // 16, split)
    own_map.wait()
    seven = pl.ds(0, GRP - 1)
    remote(maps.at[seven], maps.at[seven], (sub, grp), send_sems.at[0], recv_sems.at[0]).wait()
    map_row = jnp.concatenate([maps[g, 0:1, 0:NC] for g in range(GRP)], axis=1)

    def mark(q):
        at = lax.broadcasted_iota(jnp.int32, (128, GRP * NC), 0) + q * 128
        pick[pl.ds(pl.multiple_of(q * 128, 128), 128), :] = jnp.where(map_row == at, 1.0, 0.0).astype(BF)

    each(0, NCG // 128, mark)
    at = lax.broadcasted_iota(jnp.int32, (NC, NCG), 1)
    own_pick[...] = jnp.where(map_col[...] == at, 1.0, 0.0).astype(BF)

    arrive(back.at[0], gathered, 2, own)

    def project(t, total):
        rows = (weight[t] * unpack(gathered, t)).astype(BF)
        restricted[t] = rows
        return total + rows_times(rows, basis[t])

    local_coarse = lax.fori_loop(0, N, project, jnp.zeros((R, NC), F32), unroll=4)

    partial = gather3(jnp.dot(pieces(local_coarse), own_pick[...], preferred_element_type=F32))
    for g in range(GRP):
        part[g] = partial[:, g * SHARE : (g + 1) * SHARE]

    own = pltpu.make_async_copy(part.at[grp], part_in.at[grp], own_sems.at[3])
    own.start()

    def ring_send(source, target, k):
        def one(i):
            t = lax.rem(grp + i, GRP)
            remote(source.at[t], target.at[grp], (sub, t), send_sems.at[k], recv_sems.at[k]).start()

        each(1, GRP, one)

    def ring_wait(source, target, k):
        remote(source.at[seven], target.at[seven], (sub, grp), send_sems.at[k], recv_sems.at[k]).wait()

    def solve_local(t):
        local[t] = rows_times(restricted[t], face_inv[t])

    ring_send(part, part_in, 3)
    each(0, 48, solve_local, 4)
    own.wait()
    ring_wait(part, part_in, 3)
    share[...] = jnp.sum(part_in[...], axis=0)
    own = pltpu.make_async_copy(share, share_in.at[sub], own_sems.at[4])
    own.start()

    def share_copy(i):
        t = lax.rem(sub + i, SUB)
        remote(share, share_in.at[sub], (t, grp), send_sems.at[4], recv_sems.at[4]).start()

    each(1, SUB, share_copy)
    each(48, N, solve_local, 4)
    own.wait()
    fifteen = pl.ds(0, SUB - 1)
    remote(share_in.at[fifteen], share_in.at[fifteen], (sub, grp), send_sems.at[4], recv_sems.at[4]).wait()
    total = pieces(jnp.sum(share_in[...], axis=0))
    term = gather3(
        jnp.dot(total, coarse_high[...], preferred_element_type=F32)
        + jnp.dot(total, coarse_low[...], preferred_element_type=F32)
    )
    picked = gather3(jnp.dot(pieces(term), pick[...], preferred_element_type=F32))
    for g in range(GRP):
        chosen[g, :, 0:NC] = picked[:, g * NC : (g + 1) * NC]
        chosen[g, :, NC:128] = jnp.zeros((R, 128 - NC), F32)
    own = pltpu.make_async_copy(chosen.at[grp], chosen_in.at[grp], own_sems.at[5])
    own.start()
    ring_send(chosen, chosen_in, 5)
    own.wait()
    ring_wait(chosen, chosen_in, 5)
    mine = jnp.sum(chosen_in[...], axis=0)[:, 0:NC].astype(BF)

    def correct(t):
        value = local[t] + jnp.dot(mine, basis[t], preferred_element_type=F32)
        pack(sent.at[1], t, weight[t] * value)

    own = exchange(sent.at[1], received.at[1], 6, correct, 4)
    arrive(sent.at[1], received.at[1], 6, own)
    owner_sum(received.at[1])
    own = exchange(back.at[1], result, 7, narrow(back.at[1]), 4)
    arrive(back.at[1], result, 7, own)
    save.wait()


def extend_kernel(elem, face, coupling, res_inner, inner_inv, inner_out, face_out, rows, total):
    step = pl.program_id(0)
    steps = pl.num_programs(0)

    @pl.when(step == 0)
    def _():
        total[...] = res_inner[...].astype(F32)

    def one(i, c):
        t = step * 16 + i
        value = unpack(face, t).astype(BF)
        rows[t] = value
        e = elem[t]
        total[e] = total[e] - jnp.dot(value, coupling[i], preferred_element_type=F32)
        return c

    lax.fori_loop(0, 16, one, 0, unroll=4)

    @pl.when(step == steps - 1)
    def _():
        def inner(e, c):
            inner_out[e] = rows_times(total[e].astype(BF), inner_inv[e]).astype(BF)
            return c

        lax.fori_loop(0, E, inner, 0, unroll=4)

        def turn(q, c):
            part = rows[pl.ds(pl.multiple_of(q * 128, 128), 128)]
            face_out[...] = jnp.swapaxes(jnp.swapaxes(part, 0, 1), 1, 2)
            return c

        lax.fori_loop(0, 1, turn, 0)


def body(
    res_inner, res_face, inner_inv, face_coupling, face_elem, face_inv, coarse_basis, coarse_map, coarse_inv,
    recv_index, sharers,
):
    counts = sharers[0]
    weight = jnp.where(counts > 0, 1.0 / jnp.maximum(counts, 1).astype(F32), 0.0)
    index = recv_index[0]
    elem = face_elem[0]
    vm = pl.BlockSpec(memory_space=pltpu.VMEM)
    hbm = pl.BlockSpec(memory_space=pl.ANY)
    sm = pl.BlockSpec(memory_space=pltpu.SMEM)
    slots_last = (1, 2, 0)
    packed = (N, ROWS, 128)
    map_block = jnp.broadcast_to(jnp.pad(coarse_map, ((0, 0), (0, 128 - NC))), (8, 128))
    result, coupling = pl.pallas_call(
        main_kernel,
        out_shape=(jax.ShapeDtypeStruct(packed, BF), jax.ShapeDtypeStruct((N, B, B), BF)),
        in_specs=[hbm] * 7 + [vm] * 4 + [sm] * 2,
        out_specs=(vm, hbm),
        scratch_shapes=[
            pltpu.VMEM((E, R, B), BF),
            pltpu.VMEM((E, B, B), BF),
            pltpu.VMEM((E, R, B), BF),
            pltpu.VMEM((R, B, N), BF),
            pltpu.VMEM((N, R, B), BF),
            pltpu.VMEM((B, B, N), BF),
            pltpu.VMEM((N, B, B), BF),
            pltpu.VMEM((N, B, B), BF),
            pltpu.VMEM((NC, B, N), BF),
            pltpu.VMEM((N, NC, B), BF),
            pltpu.VMEM((SHARE, NCG), F32),
            pltpu.VMEM((SHARE, NCG), BF),
            pltpu.VMEM((SHARE, NCG), BF),
            pltpu.VMEM((NCG, GRP * NC), BF),
            pltpu.VMEM((NC, NCG), BF),
            pltpu.VMEM((GRP, 8, 128), jnp.int32),
            pltpu.VMEM((2, *packed), BF),
            pltpu.VMEM((2, *packed), BF),
            pltpu.VMEM((N * PITCH, 128), F32),
            pltpu.VMEM((N * PITCH, 128), F32),
            pltpu.VMEM((2, *packed), BF),
            pltpu.VMEM(packed, BF),
            pltpu.VMEM((N, R, B), BF),
            pltpu.VMEM((N, R, B), F32),
            pltpu.VMEM((GRP, R, SHARE), F32),
            pltpu.VMEM((GRP, R, SHARE), F32),
            pltpu.VMEM((R, SHARE), F32),
            pltpu.VMEM((SUB, R, SHARE), F32),
            pltpu.VMEM((GRP, R, 128), F32),
            pltpu.VMEM((GRP, R, 128), F32),
            pltpu.SemaphoreType.DMA((8,)),
            pltpu.SemaphoreType.DMA((8,)),
            pltpu.SemaphoreType.DMA((8,)),
            pltpu.SemaphoreType.DMA((8,)),
        ],
        name="assemble_all",
        compiler_params=pltpu.CompilerParams(
            collective_id=0, has_side_effects=True, vmem_limit_bytes=61 << 20
        ),
    )(
        res_inner,
        jnp.transpose(res_face, slots_last),
        inner_inv,
        jnp.transpose(face_coupling, slots_last),
        jnp.transpose(face_inv, slots_last),
        jnp.transpose(coarse_basis, slots_last),
        coarse_inv,
        map_block,
        coarse_map.reshape(NC, 1),
        index.reshape(1, N),
        index.reshape(N, 1),
        elem,
        weight,
    )
    whole = lambda i: (0, 0, 0)
    inner_out, face_out = pl.pallas_call(
        extend_kernel,
        grid=(N // 16,),
        out_shape=(jax.ShapeDtypeStruct((E, R, B), BF), jax.ShapeDtypeStruct((R, B, N), BF)),
        in_specs=[
            sm,
            pl.BlockSpec(packed, whole),
            pl.BlockSpec((16, B, B), lambda i: (i, 0, 0)),
            pl.BlockSpec((E, R, B), whole),
            pl.BlockSpec((E, B, B), whole),
        ],
        out_specs=(pl.BlockSpec((E, R, B), whole), pl.BlockSpec((R, B, N), whole)),
        scratch_shapes=[pltpu.VMEM((N, R, B), BF), pltpu.VMEM((E, R, B), F32)],
        name="extend",
        compiler_params=pltpu.CompilerParams(vmem_limit_bytes=40 << 20),
    )(elem, result, coupling, res_inner, inner_inv)
    return inner_out, jnp.transpose(face_out, (2, 0, 1))


def solution(mesh):
    split = P(("sub", "grp"), None, None)
    table = P(("sub", "grp"), None)
    return jax.shard_map(
        body,
        mesh=mesh,
        in_specs=(
            split, split, split, split, table, split, split, table, P("grp", None), table, table,
        ),
        out_specs=(split, split),
        check_vma=False,
    )
```

time: 212 us -> 173 us (0.82)
  Pallas kernels: 0 us -> 162 us
  blocking collectives: 96.6 us -> 0 us
  local copies, waits for them, and re-layouts: 47.7 us -> 7.47 us
  matrix products: 39.5 us -> 0 us
  waiting for transfers between devices: 14.6 us -> 0 us
  starting transfers between devices: 10.3 us -> 0 us
    pallas_call x0 -> x2, Pallas kernels: none -> 162 us  [the longest x1 145 us: body(): pl.pallas_call(main_kernel, out_shape=(jax.ShapeDtypeStruct(packed, BF),...]
    all_to_all x5 -> x0, blocking collectives: 96.6 us -> none  [the longest x2 54.2 us: send_out(): lax.all_to_all(partials, ('sub', 'grp'), split_axis=0, concat_axis=0, til...]
    dot_general x13 -> x0, matrix products: 39.5 us -> none  [the longest x1 6.75 us: body(): jnp.einsum('lrb,lcb->lrc', nearby, face_coupling, preferred_element_type=...]
    unnamed x17 -> x8, local copies, waits for them, and re-layouts: 37.5 us -> 3.47 us
    all_to_all x2 -> x0, waiting for transfers between devices: 14.6 us -> none  [the longest x1 12.7 us: send_back(): lax.all_to_all(spread, ('sub', 'grp'), split_axis=0, concat_axis=0, tiled...]
    all_to_all x2 -> x0, starting transfers between devices: 10.3 us -> none  [the longest x1 5.75 us: copy_for_each(): lax.all_to_all(jnp.broadcast_to(x[None], (size, *x.shape)), axis, 0, 0, t...]
    all_to_all x2 -> x0, local copies, waits for them, and re-layouts: 2.53 us -> none  [send_out(): lax.all_to_all(partials, ('sub', 'grp'), split_axis=0, concat_axis=0, til...]
  transfers between devices with their start and end apart: 2 -> 0, of which waited for: 2 -> 0; matrix products, arithmetic and copies ran while one was open for 9% -> 0% of each run, Pallas kernels for 0% -> 0%
where the time goes in v2:
time: 173 us; the launch traced here: 172 us
  Pallas kernels  162 us (94%)
  local copies, waits for them, and re-layouts  7.47 us (4%)
    pallas_call x1, Pallas kernels, body(): pl.pallas_call(main_kernel, out_shape=(jax.ShapeDtypeStruct(packed, BF),...  145 us
    pallas_call x1, Pallas kernels, body(): pl.pallas_call(extend_kernel, grid=(N // 16,), out_shape=(jax.ShapeDtypeS...  17.4 us
    unnamed x8, local copies, waits for them, and re-layouts  3.47 us

profile of v2, /device:TPU:1, one launch (start us, length us, event | category | flops | bytes accessed | tf_op | source)
XLA Modules:
  0.0 171.8 jit_solution(8913548852905541914)
XLA Ops:
  0.6 1.2 fusion.weight
  1.8 0.7 pad_bitcast_fusion
  2.5 0.6 broadcast_in_dim.12.map_block
  3.1 1.4 copy.13.map_col
  4.4 1.4 copy.14.index_col
  5.8 0.0 copy-start.1
  5.8 0.0 copy-start.3
  5.8 145.0 %assemble_all.1 = (bf16[128,18,128]{2,1,0:T(8,128)(2,1)}, bf16[128,144,144]{2,1,0:T(8,128)(2,1)}) custom-call(bf16[64,16,144]{2,1,0:T(8,128)(2,1)} %res_inner.1, bf16[16,144,128]{2,1,0:T(8,128)(2,1)} %bitcast.17, bf16[64,144,144]{2,1,0:T(8,128)(2,1)} %inner_inv.1, bf16[144,144,128]{2,1,0:T(8,128)(2,1)} %bitcast.14, bf16[144,144,128]{2,1,0:T(8,128)(2,1)} %bitcast.15, ...), custom_call_target="tpu_custom_call" | custom-call | tf_op jit(solution)/shard_map/assemble_all/pallas_call | solution.py:344
  150.9 0.0 copy-done.1
  150.9 0.0 copy-done.3
  150.9 0.0 copy-start
  150.9 2.3 %copy-done = bf16[64,144,144]{2,1,0:T(8,128)(2,1)S(1)} copy-done((bf16[64,144,144]{2,1,0:T(8,128)(2,1)S(1)}, bf16[64,144,144]{2,1,0:T(8,128)(2,1)}, u32[]{:S(2)}) %copy-start) | copy-done | bytes 2654232
  153.2 0.0 copy-start.2
  153.2 1.1 copy-done.2
  154.4 17.4 %extend.1 = (bf16[64,16,144]{2,1,0:T(8,128)(2,1)}, bf16[16,144,128]{2,1,0:T(8,128)(2,1)}) custom-call(s32[128]{0:T(128)S(1)} %bitcast.13, bf16[128,18,128]{2,1,0:T(8,128)(2,1)S(1)} %copy-done.2, bf16[128,144,144]{2,1,0:T(8,128)(2,1)} %get-tuple-element.7.coupling, bf16[64,16,144]{2,1,0:T(8,128)(2,1)S(1)} %copy-done.1, bf16[64,144,144]{2,1,0:T(8,128)(2,1)S(1)} %copy-done), custom_call_target="tpu_custom_call" | custom-call | tf_op jit(solution)/shard_map/extend/pallas_call | solution.py:405
Async XLA Ops:
  5.8 145.0 %copy-start.1 = (bf16[64,16,144]{2,1,0:T(8,128)(2,1)S(1)}, bf16[64,16,144]{2,1,0:T(8,128)(2,1)}, u32[]{:S(2)}) copy-start(bf16[64,16,144]{2,1,0:T(8,128)(2,1)} %res_inner.1) | copy-start | bytes 884740
  5.8 145.0 %copy-start.3 = (s32[1,128]{1,0:T(1,128)S(1)}, s32[1,128]{1,0:T(1,128)}, u32[]{:S(2)}) copy-start(s32[1,128]{1,0:T(1,128)} %param.15) | copy-start | bytes 1540
  150.9 2.3 %copy-start = (bf16[64,144,144]{2,1,0:T(8,128)(2,1)S(1)}, bf16[64,144,144]{2,1,0:T(8,128)(2,1)}, u32[]{:S(2)}) copy-start(bf16[64,144,144]{2,1,0:T(8,128)(2,1)} %inner_inv.1) | copy-start | bytes 7962628
  153.2 1.1 copy-start.2

commit v3 on v2

--- a/solution.py
+++ b/solution.py
@@ -31,24 +31,21 @@
     )
 
 
-def own_group():
+def pack(out, t, value):
+    out[t, 0:R, :] = value[:, 0:128].astype(BF)
     row = lax.broadcasted_iota(jnp.int32, (R, 128), 0)
     lane = lax.broadcasted_iota(jnp.int32, (R, 128), 1)
-    return (row % 8) == (lane // 16)
-
-
-def pack(out, t, value):
-    out[t, 0:R, :] = value[:, 0:128].astype(BF)
-    tail = jnp.where(own_group(), jnp.concatenate([value[:, 128:B]] * 8, axis=1), 0.0)
+    tail = jnp.concatenate([value[:, 128:B], jnp.zeros((R, 112), F32)], axis=1)
+    for shift in (16, 32, 64):
+        tail = tail + pltpu.roll(tail, shift, 1)
+    tail = jnp.where((row + lane // 16) % 8 == 0, tail, 0.0)
     out[t, R:ROWS, :] = jnp.sum(tail.reshape(2, 8, 128), axis=1).astype(BF)
 
 
 def unpack(ref, t):
     tail = ref[t, R:ROWS, :].astype(F32)
     tail = jnp.broadcast_to(tail[:, None, :], (2, 8, 128)).reshape(R, 128)
-    tail = jnp.where(own_group(), tail, 0.0)
-    for shift in (64, 32, 16):
-        tail = tail + pltpu.roll(tail, shift, 1)
+    tail = pltpu.roll(tail, 0, 1, stride=16, stride_axis=0)
     return jnp.concatenate([ref[t, 0:R, :].astype(F32), tail[:, 0:16]], axis=1)
 
 
@@ -70,13 +67,13 @@
 
 def main_kernel(
     res_inner_h, res_face_h, inner_inv_h, coupling_h, face_inv_h, basis_h, coarse_inv_h,
-    map_block, map_col, index_row, index_col, elem, weight,
+    map_row_own, index_row, sharers, elem,
     result, coupling_out,
     res_inner, inner_inv, inner_w, res_face, face_rows, stage, coupling, face_inv, basis_stage, basis,
     coarse_inv, coarse_high, coarse_low, pick, own_pick, maps,
     sent, received, wide, wide2, back, gathered, restricted, local,
-    part, part_in, share, share_in, chosen, chosen_in,
-    load_sems, send_sems, recv_sems, own_sems,
+    part, part_in, share, share_in, chosen, chosen_in, map_block, weight, contrast,
+    entered, load_sems, send_sems, recv_sems, own_sems,
 ):
     sub = lax.axis_index("sub")
     grp = lax.axis_index("grp")
@@ -88,28 +85,40 @@
 
     load(res_inner_h, res_inner, 0).start()
     load(inner_inv_h, inner_inv, 1).start()
-    load(coupling_h, stage, 2).start()
-    load(res_face_h, res_face, 3).start()
-    load(basis_h, basis_stage, 4).start()
-    load(coarse_inv_h, coarse_inv, 5).start()
-
-    def greet(i):
-        pl.semaphore_signal(barrier, inc=1, device_id=place(lax.rem(me + i, N)), device_id_type=MESH)
-
-    def inner(e, c):
+
+    def signal(semaphore, device):
+        pl.semaphore_signal(semaphore, inc=1, device_id=device, device_id_type=MESH)
+
+    def each(first, last, f, unroll=1):
+        def one(i, c):
+            f(i)
+            return c
+
+        lax.fori_loop(first, last, one, 0, unroll=unroll)
+
+    each(1, GRP, lambda i: signal(barrier, (sub, lax.rem(grp + i, GRP))))
+    each(1, SUB, lambda i: signal(barrier, (lax.rem(sub + i, SUB), grp)))
+
+    def tall(row):
+        return jnp.broadcast_to(row, (N, N)).T
+
+    counts = sharers[...]
+    weight[...] = tall(jnp.where(counts > 0, 1.0 / jnp.maximum(counts, 1).astype(F32), 0.0))
+    map_own = jnp.concatenate([map_row_own[...], jnp.zeros((1, 128 - NC), jnp.int32)], axis=1)
+    map_block[...] = jnp.broadcast_to(map_own, (8, 128))
+    index = index_row[...].astype(F32)
+    contrast[...] = jnp.where((index == tall(index)) & (index < 32.0), 1.0, 0.0).astype(BF)
+
+    def inner(e):
         inner_w[e] = rows_times(res_inner[e], inner_inv[e]).astype(BF)
-        return c
-
-    def inner_greet(e, c):
-        greet(2 * e)
-        greet(2 * e + 1)
-        return inner(e, c)
 
     load(res_inner_h, res_inner, 0).wait()
     load(inner_inv_h, inner_inv, 1).wait()
-    greet(1)
-    inner(0, 0)
-    lax.fori_loop(1, E, inner_greet, 0, unroll=3)
+    load(res_face_h, res_face, 3).start()
+    load(coupling_h, stage, 2).start()
+    each(0, E, inner, 8)
+    pl.semaphore_wait(barrier, GRP + SUB - 2)
+    each(1, SUB, lambda i: signal(entered, (lax.rem(sub + i, SUB), grp)))
 
     def turn(src, dst, q):
         part_rows = src[pl.ds(pl.multiple_of(q * 16, 16), 16)]
@@ -128,36 +137,42 @@
     load(coupling_h, stage, 2).wait()
     turns(stage, coupling, 0, 9)
     load(face_inv_h, stage, 6).start()
+    load(basis_h, basis_stage, 4).start()
+    load(coarse_inv_h, coarse_inv, 5).start()
     save = load(coupling, coupling_out, 7)
     save.start()
 
-    pl.semaphore_wait(barrier, N - 1)
+    pl.semaphore_wait(entered, SUB - 1)
 
     def map_copy(i):
         return remote(map_block, maps.at[grp], (sub, lax.rem(grp + i, GRP)), send_sems.at[0], recv_sems.at[0])
-
-    def each(first, last, f, unroll=1):
-        def one(i, c):
-            f(i)
-            return c
-
-        lax.fori_loop(first, last, one, 0, unroll=unroll)
 
     own_map = pltpu.make_async_copy(map_block, maps.at[grp], own_sems.at[0])
     own_map.start()
     each(1, GRP, lambda i: map_copy(i).start())
 
-    def exchange(source, target, k, fill, unroll):
-        fill(me)
+    def quad(i):
+        return lax.rem(me // 4 + i, N // 4) * 4
+
+    def exchange(source, target, k, fill):
+        def give(t):
+            remote(source.at[t], target.at[me], place(t), send_sems.at[k], recv_sems.at[k]).start()
+
+        def batch(q):
+            for i in range(4):
+                fill(quad(q * 4 + i))
+
+        batch(0)
         own = pltpu.make_async_copy(source.at[me], target.at[me], own_sems.at[k])
         own.start()
-
-        def one(i):
-            t = lax.rem(me + i, N)
-            fill(t)
-            remote(source.at[t], target.at[me], place(t), send_sems.at[k], recv_sems.at[k]).start()
-
-        each(1, N, one, unroll)
+        each(1, 4, lambda j: give(quad(0) + lax.rem(me + j, 4)))
+        each(4, 16, lambda j: give(quad(j // 4) + lax.rem(me + j, 4)))
+
+        def more(q):
+            batch(q)
+            each(16 * q, 16 * q + 16, lambda j: give(quad(j // 4) + lax.rem(me + j, 4)))
+
+        each(1, N // 16, more)
         return own
 
     def arrive(source, target, k, own):
@@ -165,34 +180,40 @@
         rest = pl.ds(0, N - 1)
         remote(source.at[rest], target.at[rest], (sub, grp), send_sems.at[k], recv_sems.at[k]).wait()
 
-    def condense(t):
-        product = rows_times(inner_w[elem[t]], coupling[t])
-        pack(sent.at[0], t, weight[t] * (face_rows[t].astype(F32) - product))
-
-    own = exchange(sent.at[0], received.at[0], 1, condense, 4)
+    def scaled(t, value):
+        scale = jnp.broadcast_to(weight[pl.ds(t, 1), :], (R, 128))
+        return jnp.concatenate([scale, scale[:, 0:16]], axis=1) * value
+
+    def condense(base):
+        for t in [base + k for k in range(4)]:
+            product = rows_times(inner_w[elem[0, t]], coupling[t])
+            pack(sent.at[0], t, scaled(t, face_rows[t].astype(F32) - product))
+
+    own = exchange(sent.at[0], received.at[0], 1, condense)
     load(face_inv_h, stage, 6).wait()
     turns(stage, face_inv, 0, 4)
     arrive(sent.at[0], received.at[0], 1, own)
 
-    same = jnp.where((index_row[...] == index_col[...]) & (index_row[...] < 32), 1.0, 0.0).astype(BF)
+    same = contrast[...]
 
     def owner_sum(source):
         def widen(s):
             wide[pl.ds(pl.multiple_of(s * PITCH, 8), ROWS)] = source[s].astype(F32)
 
-        each(0, N, widen, 4)
+        each(0, N, widen, 8)
         for k in range(ROWS):
             rows = wide[pl.ds(k, N, stride=PITCH), :].astype(BF)
             wide2[pl.ds(k, N, stride=PITCH), :] = jnp.dot(same, rows, preferred_element_type=F32)
 
     def narrow(target):
-        def one(t):
-            target[t] = wide2[pl.ds(pl.multiple_of(t * PITCH, 8), ROWS)].astype(BF)
+        def one(base):
+            for t in [base + k for k in range(4)]:
+                target[t] = wide2[pl.ds(pl.multiple_of(t * PITCH, 8), ROWS)].astype(BF)
 
         return one
 
     owner_sum(received.at[0])
-    own = exchange(back.at[0], gathered, 2, narrow(back.at[0]), 4)
+    own = exchange(back.at[0], gathered, 2, narrow(back.at[0]))
 
     turns(stage, face_inv, 4, 9)
     load(basis_h, basis_stage, 4).wait()
@@ -216,17 +237,25 @@
         pick[pl.ds(pl.multiple_of(q * 128, 128), 128), :] = jnp.where(map_row == at, 1.0, 0.0).astype(BF)
 
     each(0, NCG // 128, mark)
-    at = lax.broadcasted_iota(jnp.int32, (NC, NCG), 1)
-    own_pick[...] = jnp.where(map_col[...] == at, 1.0, 0.0).astype(BF)
+    map_tall = tall(map_own.astype(F32))[0:NC]
+    for q in range(NCG // 128):
+        at = (lax.broadcasted_iota(jnp.int32, (NC, 128), 1) + q * 128).astype(F32)
+        own_pick[:, q * 128 : (q + 1) * 128] = jnp.where(map_tall == at, 1.0, 0.0).astype(BF)
 
     arrive(back.at[0], gathered, 2, own)
 
-    def project(t, total):
-        rows = (weight[t] * unpack(gathered, t)).astype(BF)
-        restricted[t] = rows
-        return total + rows_times(rows, basis[t])
-
-    local_coarse = lax.fori_loop(0, N, project, jnp.zeros((R, NC), F32), unroll=4)
+    def basis4(q):
+        return basis[pl.ds(pl.multiple_of(q * 4, 4), 4)].reshape(4 * NC, B)
+
+    def project(q, total):
+        rows = []
+        for t in [4 * q + k for k in range(4)]:
+            rows.append(scaled(t, unpack(gathered, t)).astype(BF))
+            restricted[t] = rows[-1]
+        return total + rows_times(jnp.concatenate(rows, axis=0), basis4(q))
+
+    crossed = lax.fori_loop(0, N // 4, project, jnp.zeros((4 * R, 4 * NC), F32), unroll=2)
+    local_coarse = sum(crossed[k * R : (k + 1) * R, k * NC : (k + 1) * NC] for k in range(4))
 
     partial = gather3(jnp.dot(pieces(local_coarse), own_pick[...], preferred_element_type=F32))
     for g in range(GRP):
@@ -249,7 +278,7 @@
         local[t] = rows_times(restricted[t], face_inv[t])
 
     ring_send(part, part_in, 3)
-    each(0, 48, solve_local, 4)
+    each(0, 64, solve_local, 8)
     own.wait()
     ring_wait(part, part_in, 3)
     share[...] = jnp.sum(part_in[...], axis=0)
@@ -261,7 +290,7 @@
         remote(share, share_in.at[sub], (t, grp), send_sems.at[4], recv_sems.at[4]).start()
 
     each(1, SUB, share_copy)
-    each(48, N, solve_local, 4)
+    each(64, N, solve_local, 8)
     own.wait()
     fifteen = pl.ds(0, SUB - 1)
     remote(share_in.at[fifteen], share_in.at[fifteen], (sub, grp), send_sems.at[4], recv_sems.at[4]).wait()
@@ -279,72 +308,81 @@
     ring_send(chosen, chosen_in, 5)
     own.wait()
     ring_wait(chosen, chosen_in, 5)
-    mine = jnp.sum(chosen_in[...], axis=0)[:, 0:NC].astype(BF)
-
-    def correct(t):
-        value = local[t] + jnp.dot(mine, basis[t], preferred_element_type=F32)
-        pack(sent.at[1], t, weight[t] * value)
-
-    own = exchange(sent.at[1], received.at[1], 6, correct, 4)
+    mine = jnp.sum(chosen_in[...], axis=0)[:, 0:NC]
+    row = lax.broadcasted_iota(jnp.int32, (4 * R, 4 * NC), 0) // R
+    lane = lax.broadcasted_iota(jnp.int32, (4 * R, 4 * NC), 1) // NC
+    mine4 = jnp.concatenate([jnp.concatenate([mine] * 4, axis=1)] * 4, axis=0)
+    mine4 = jnp.where(row == lane, mine4, 0.0).astype(BF)
+
+    def correct(base):
+        coarse = jnp.dot(mine4, basis4(base // 4), preferred_element_type=F32)
+        for k in range(4):
+            pack(sent.at[1], base + k, scaled(base + k, local[base + k] + coarse[k * R : (k + 1) * R]))
+
+    own = exchange(sent.at[1], received.at[1], 6, correct)
     arrive(sent.at[1], received.at[1], 6, own)
     owner_sum(received.at[1])
-    own = exchange(back.at[1], result, 7, narrow(back.at[1]), 4)
+    own = exchange(back.at[1], result, 7, narrow(back.at[1]))
     arrive(back.at[1], result, 7, own)
     save.wait()
 
 
-def extend_kernel(elem, face, coupling, res_inner, inner_inv, inner_out, face_out, rows, total):
+def extend_kernel(elem, face, coupling, res_inner_h, inner_inv_h, inner_out, face_out, rows, total, terms, res_inner, inner_inv, sems):
     step = pl.program_id(0)
     steps = pl.num_programs(0)
+    first = pltpu.make_async_copy(res_inner_h, res_inner, sems.at[0])
+    second = pltpu.make_async_copy(inner_inv_h, inner_inv, sems.at[1])
 
     @pl.when(step == 0)
     def _():
+        first.start()
+        second.start()
+
+    def one(i, c):
+        value = unpack(face, step * 16 + i).astype(BF)
+        rows[step * 16 + i] = value
+        terms[i] = jnp.dot(value, coupling[i], preferred_element_type=F32)
+        return c
+
+    lax.fori_loop(0, 16, one, 0, unroll=16)
+
+    @pl.when(step == 0)
+    def _():
+        first.wait()
         total[...] = res_inner[...].astype(F32)
 
-    def one(i, c):
-        t = step * 16 + i
-        value = unpack(face, t).astype(BF)
-        rows[t] = value
-        e = elem[t]
-        total[e] = total[e] - jnp.dot(value, coupling[i], preferred_element_type=F32)
+    def add(i, c):
+        e = elem[0, step * 16 + i]
+        total[e] = total[e] - terms[i]
         return c
 
-    lax.fori_loop(0, 16, one, 0, unroll=4)
+    lax.fori_loop(0, 16, add, 0, unroll=4)
 
     @pl.when(step == steps - 1)
     def _():
+        second.wait()
+
         def inner(e, c):
             inner_out[e] = rows_times(total[e].astype(BF), inner_inv[e]).astype(BF)
             return c
 
-        lax.fori_loop(0, E, inner, 0, unroll=4)
-
-        def turn(q, c):
-            part = rows[pl.ds(pl.multiple_of(q * 128, 128), 128)]
-            face_out[...] = jnp.swapaxes(jnp.swapaxes(part, 0, 1), 1, 2)
-            return c
-
-        lax.fori_loop(0, 1, turn, 0)
+        lax.fori_loop(0, E, inner, 0, unroll=8)
+        face_out[...] = jnp.swapaxes(jnp.swapaxes(rows[...], 0, 1), 1, 2)
 
 
 def body(
     res_inner, res_face, inner_inv, face_coupling, face_elem, face_inv, coarse_basis, coarse_map, coarse_inv,
     recv_index, sharers,
 ):
-    counts = sharers[0]
-    weight = jnp.where(counts > 0, 1.0 / jnp.maximum(counts, 1).astype(F32), 0.0)
-    index = recv_index[0]
-    elem = face_elem[0]
     vm = pl.BlockSpec(memory_space=pltpu.VMEM)
     hbm = pl.BlockSpec(memory_space=pl.ANY)
     sm = pl.BlockSpec(memory_space=pltpu.SMEM)
     slots_last = (1, 2, 0)
     packed = (N, ROWS, 128)
-    map_block = jnp.broadcast_to(jnp.pad(coarse_map, ((0, 0), (0, 128 - NC))), (8, 128))
     result, coupling = pl.pallas_call(
         main_kernel,
         out_shape=(jax.ShapeDtypeStruct(packed, BF), jax.ShapeDtypeStruct((N, B, B), BF)),
-        in_specs=[hbm] * 7 + [vm] * 4 + [sm] * 2,
+        in_specs=[hbm] * 7 + [vm] * 3 + [sm],
         out_specs=(vm, hbm),
         scratch_shapes=[
             pltpu.VMEM((E, R, B), BF),
@@ -377,6 +415,10 @@
             pltpu.VMEM((SUB, R, SHARE), F32),
             pltpu.VMEM((GRP, R, 128), F32),
             pltpu.VMEM((GRP, R, 128), F32),
+            pltpu.VMEM((8, 128), jnp.int32),
+            pltpu.VMEM((N, N), F32),
+            pltpu.VMEM((N, N), BF),
+            pltpu.SemaphoreType.REGULAR,
             pltpu.SemaphoreType.DMA((8,)),
             pltpu.SemaphoreType.DMA((8,)),
             pltpu.SemaphoreType.DMA((8,)),
@@ -394,12 +436,10 @@
         jnp.transpose(face_inv, slots_last),
         jnp.transpose(coarse_basis, slots_last),
         coarse_inv,
-        map_block,
-        coarse_map.reshape(NC, 1),
-        index.reshape(1, N),
-        index.reshape(N, 1),
-        elem,
-        weight,
+        coarse_map,
+        recv_index,
+        sharers,
+        face_elem,
     )
     whole = lambda i: (0, 0, 0)
     inner_out, face_out = pl.pallas_call(
@@ -410,14 +450,21 @@
             sm,
             pl.BlockSpec(packed, whole),
             pl.BlockSpec((16, B, B), lambda i: (i, 0, 0)),
-            pl.BlockSpec((E, R, B), whole),
-            pl.BlockSpec((E, B, B), whole),
+            hbm,
+            hbm,
         ],
         out_specs=(pl.BlockSpec((E, R, B), whole), pl.BlockSpec((R, B, N), whole)),
-        scratch_shapes=[pltpu.VMEM((N, R, B), BF), pltpu.VMEM((E, R, B), F32)],
+        scratch_shapes=[
+            pltpu.VMEM((N, R, B), BF),
+            pltpu.VMEM((E, R, B), F32),
+            pltpu.VMEM((16, R, B), F32),
+            pltpu.VMEM((E, R, B), BF),
+            pltpu.VMEM((E, B, B), BF),
+            pltpu.SemaphoreType.DMA((2,)),
+        ],
         name="extend",
-        compiler_params=pltpu.CompilerParams(vmem_limit_bytes=40 << 20),
-    )(elem, result, coupling, res_inner, inner_inv)
+        compiler_params=pltpu.CompilerParams(vmem_limit_bytes=60 << 20),
+    )(face_elem, result, coupling, res_inner, inner_inv)
     return inner_out, jnp.transpose(face_out, (2, 0, 1))
 
 

time: 173 us -> 111 us (0.64)
  Pallas kernels: 162 us -> 110 us
  local copies, waits for them, and re-layouts: 7.47 us -> 0 us
    pallas_call x1, Pallas kernels: 145 us -> 98 us  [body(): pl.pallas_call(main_kernel, out_shape=(jax.ShapeDtypeStruct(packed, BF),...]
    pallas_call x1, Pallas kernels: 17.4 us -> 12.5 us  [body(): pl.pallas_call(extend_kernel, grid=(N // 16,), out_shape=(jax.ShapeDtypeS...]
    unnamed x8 -> x0, local copies, waits for them, and re-layouts: 3.47 us -> none
where the time goes in v3:
time: 111 us
  Pallas kernels  110 us (99%)
    pallas_call x1, Pallas kernels, body(): pl.pallas_call(main_kernel, out_shape=(jax.ShapeDtypeStruct(packed, BF),...  98 us
    pallas_call x1, Pallas kernels, body(): pl.pallas_call(extend_kernel, grid=(N // 16,), out_shape=(jax.ShapeDtypeS...  12.5 us

profile of v3, /device:TPU:1, one launch (start us, length us, event | category | flops | bytes accessed | tf_op | source)
XLA Modules:
  0.0 111.1 jit_solution(3164121425241330227)
XLA Ops:
  0.6 98.0 %assemble_all.1 = (bf16[128,18,128]{2,1,0:T(8,128)(2,1)}, bf16[128,144,144]{2,1,0:T(8,128)(2,1)}) custom-call(bf16[64,16,144]{2,1,0:T(8,128)(2,1)} %res_inner_h.3, bf16[16,144,128]{2,1,0:T(8,128)(2,1)} %bitcast.8, bf16[64,144,144]{2,1,0:T(8,128)(2,1)} %inner_inv_h.3, bf16[144,144,128]{2,1,0:T(8,128)(2,1)} %bitcast.5, bf16[144,144,128]{2,1,0:T(8,128)(2,1)} %bitcast.6, ...), custom_call_target="tpu_custom_call" | custom-call | tf_op jit(solution)/shard_map/assemble_all/pallas_call | solution.py:382
  98.6 12.5 %extend.1 = (bf16[64,16,144]{2,1,0:T(8,128)(2,1)}, bf16[16,144,128]{2,1,0:T(8,128)(2,1)}) custom-call(s32[1,128]{1,0:T(1,128)} %elem.3, bf16[128,18,128]{2,1,0:T(8,128)(2,1)} %get-tuple-element.6.face, bf16[128,144,144]{2,1,0:T(8,128)(2,1)} %get-tuple-element.7.coupling, bf16[64,16,144]{2,1,0:T(8,128)(2,1)} %res_inner_h.3, bf16[64,144,144]{2,1,0:T(8,128)(2,1)} %inner_inv_h.3), custom_call_target="tpu_custom_call" | custom-call | tf_op jit(solution)/shard_map/extend/pallas_call | solution.py:445

commit v4 on v3

--- a/solution.py
+++ b/solution.py
@@ -68,12 +68,12 @@
 def main_kernel(
     res_inner_h, res_face_h, inner_inv_h, coupling_h, face_inv_h, basis_h, coarse_inv_h,
     map_row_own, index_row, sharers, elem,
-    result, coupling_out,
+    rows_out, terms_out,
     res_inner, inner_inv, inner_w, res_face, face_rows, stage, coupling, face_inv, basis_stage, basis,
     coarse_inv, coarse_high, coarse_low, pick, own_pick, maps,
-    sent, received, wide, wide2, back, gathered, restricted, local,
+    sent, received, wide, wide2, back, gathered, gathered2, restricted, local,
     part, part_in, share, share_in, chosen, chosen_in, map_block, weight, contrast,
-    entered, load_sems, send_sems, recv_sems, own_sems,
+    entered, piece_sems, batch_sems, load_sems, send_sems, recv_sems, own_sems,
 ):
     sub = lax.axis_index("sub")
     grp = lax.axis_index("grp")
@@ -84,7 +84,22 @@
         return pltpu.make_async_copy(src, dst, load_sems.at[k])
 
     load(res_inner_h, res_inner, 0).start()
-    load(inner_inv_h, inner_inv, 1).start()
+
+    def piece(src, dst, q, k):
+        rows = pl.ds(pl.multiple_of(q * 16, 16), 16)
+        return pltpu.make_async_copy(src.at[rows], dst.at[rows], piece_sems.at[k + q])
+
+    def inverse_piece(q):
+        return piece(inner_inv_h, inner_inv, q, 0)
+
+    def coupling_piece(q):
+        return piece(coupling_h, stage, q, 4)
+
+    for q in range(4):
+        inverse_piece(q).start()
+    load(res_face_h, res_face, 3).start()
+    for q in range(9):
+        coupling_piece(q).start()
 
     def signal(semaphore, device):
         pl.semaphore_signal(semaphore, inc=1, device_id=device, device_id_type=MESH)
@@ -113,10 +128,13 @@
         inner_w[e] = rows_times(res_inner[e], inner_inv[e]).astype(BF)
 
     load(res_inner_h, res_inner, 0).wait()
-    load(inner_inv_h, inner_inv, 1).wait()
-    load(res_face_h, res_face, 3).start()
-    load(coupling_h, stage, 2).start()
-    each(0, E, inner, 8)
+
+    def inners(q):
+        inverse_piece(q).wait()
+        for e in range(16):
+            inner(16 * q + e)
+
+    each(0, 4, inners)
     pl.semaphore_wait(barrier, GRP + SUB - 2)
     each(1, SUB, lambda i: signal(entered, (lax.rem(sub + i, SUB), grp)))
 
@@ -134,13 +152,15 @@
 
     load(res_face_h, res_face, 3).wait()
     turns(res_face, face_rows, 0, 1)
-    load(coupling_h, stage, 2).wait()
-    turns(stage, coupling, 0, 9)
+
+    def coupling_turn(q):
+        coupling_piece(q).wait()
+        turn(stage, coupling, q)
+
+    each(0, 9, coupling_turn)
     load(face_inv_h, stage, 6).start()
     load(basis_h, basis_stage, 4).start()
     load(coarse_inv_h, coarse_inv, 5).start()
-    save = load(coupling, coupling_out, 7)
-    save.start()
 
     pl.semaphore_wait(entered, SUB - 1)
 
@@ -154,9 +174,9 @@
     def quad(i):
         return lax.rem(me // 4 + i, N // 4) * 4
 
-    def exchange(source, target, k, fill):
-        def give(t):
-            remote(source.at[t], target.at[me], place(t), send_sems.at[k], recv_sems.at[k]).start()
+    def exchange(source, target, k, fill, arrived):
+        def give(t, q):
+            remote(source.at[t], target.at[me], place(t), send_sems.at[k], arrived(q)).start()
 
         def batch(q):
             for i in range(4):
@@ -165,20 +185,49 @@
         batch(0)
         own = pltpu.make_async_copy(source.at[me], target.at[me], own_sems.at[k])
         own.start()
-        each(1, 4, lambda j: give(quad(0) + lax.rem(me + j, 4)))
-        each(4, 16, lambda j: give(quad(j // 4) + lax.rem(me + j, 4)))
+        each(1, 4, lambda j: give(quad(0) + lax.rem(me + j, 4), 0))
+        each(4, 16, lambda j: give(quad(j // 4) + lax.rem(me + j, 4), 0))
 
         def more(q):
             batch(q)
-            each(16 * q, 16 * q + 16, lambda j: give(quad(j // 4) + lax.rem(me + j, 4)))
+            each(16 * q, 16 * q + 16, lambda j: give(quad(j // 4) + lax.rem(me + j, 4), q))
 
         each(1, N // 16, more)
         return own
 
+    def all_at_once(k):
+        return lambda q: recv_sems.at[k]
+
+    def in_batches(c):
+        return lambda q: batch_sems.at[c * 8 + q]
+
+    def sent_all(source, k):
+        rest = source.at[pl.ds(0, N - 1)]
+        remote(rest, rest, (sub, grp), send_sems.at[k], recv_sems.at[k]).wait_send()
+
     def arrive(source, target, k, own):
         own.wait()
-        rest = pl.ds(0, N - 1)
-        remote(source.at[rest], target.at[rest], (sub, grp), send_sems.at[k], recv_sems.at[k]).wait()
+        rest = target.at[pl.ds(0, N - 1)]
+        remote(rest, rest, (sub, grp), send_sems.at[k], recv_sems.at[k]).wait_recv()
+        sent_all(source, k)
+
+    def arrive_in_batches(source, target, k, own, arrived, use, carry):
+        def wait(q, count):
+            some = target.at[pl.ds(0, count)]
+            remote(some, some, (sub, grp), send_sems.at[k], arrived(q)).wait_recv()
+
+        def use_batch(q, carry):
+            return use([quad(N // 4 - 4 * q - i) for i in range(4)], carry)
+
+        def next_batch(q, carry):
+            wait(q, 16)
+            return use_batch(q, carry)
+
+        own.wait()
+        wait(0, 15)
+        carry = lax.fori_loop(1, N // 16, next_batch, use_batch(0, carry))
+        sent_all(source, k)
+        return carry
 
     def scaled(t, value):
         scale = jnp.broadcast_to(weight[pl.ds(t, 1), :], (R, 128))
@@ -187,12 +236,12 @@
     def condense(base):
         for t in [base + k for k in range(4)]:
             product = rows_times(inner_w[elem[0, t]], coupling[t])
-            pack(sent.at[0], t, scaled(t, face_rows[t].astype(F32) - product))
-
-    own = exchange(sent.at[0], received.at[0], 1, condense)
+            pack(sent, t, scaled(t, face_rows[t].astype(F32) - product))
+
+    own = exchange(sent, received.at[0], 1, condense, all_at_once(1))
     load(face_inv_h, stage, 6).wait()
     turns(stage, face_inv, 0, 4)
-    arrive(sent.at[0], received.at[0], 1, own)
+    arrive(sent, received.at[0], 1, own)
 
     same = contrast[...]
 
@@ -213,7 +262,7 @@
         return one
 
     owner_sum(received.at[0])
-    own = exchange(back.at[0], gathered, 2, narrow(back.at[0]))
+    own = exchange(back, gathered, 2, narrow(back), in_batches(0))
 
     turns(stage, face_inv, 4, 9)
     load(basis_h, basis_stage, 4).wait()
@@ -242,19 +291,21 @@
         at = (lax.broadcasted_iota(jnp.int32, (NC, 128), 1) + q * 128).astype(F32)
         own_pick[:, q * 128 : (q + 1) * 128] = jnp.where(map_tall == at, 1.0, 0.0).astype(BF)
 
-    arrive(back.at[0], gathered, 2, own)
-
     def basis4(q):
         return basis[pl.ds(pl.multiple_of(q * 4, 4), 4)].reshape(4 * NC, B)
 
-    def project(q, total):
-        rows = []
-        for t in [4 * q + k for k in range(4)]:
-            rows.append(scaled(t, unpack(gathered, t)).astype(BF))
-            restricted[t] = rows[-1]
-        return total + rows_times(jnp.concatenate(rows, axis=0), basis4(q))
-
-    crossed = lax.fori_loop(0, N // 4, project, jnp.zeros((4 * R, 4 * NC), F32), unroll=2)
+    def project(bases, total):
+        for base in bases:
+            rows = []
+            for t in [base + k for k in range(4)]:
+                rows.append(scaled(t, unpack(gathered, t)).astype(BF))
+                restricted[t] = rows[-1]
+            total = total + rows_times(jnp.concatenate(rows, axis=0), basis4(base // 4))
+        return total
+
+    crossed = arrive_in_batches(
+        back, gathered, 2, own, in_batches(0), project, jnp.zeros((4 * R, 4 * NC), F32)
+    )
     local_coarse = sum(crossed[k * R : (k + 1) * R, k * NC : (k + 1) * NC] for k in range(4))
 
     partial = gather3(jnp.dot(pieces(local_coarse), own_pick[...], preferred_element_type=F32))
@@ -317,57 +368,51 @@
     def correct(base):
         coarse = jnp.dot(mine4, basis4(base // 4), preferred_element_type=F32)
         for k in range(4):
-            pack(sent.at[1], base + k, scaled(base + k, local[base + k] + coarse[k * R : (k + 1) * R]))
-
-    own = exchange(sent.at[1], received.at[1], 6, correct)
-    arrive(sent.at[1], received.at[1], 6, own)
+            pack(sent, base + k, scaled(base + k, local[base + k] + coarse[k * R : (k + 1) * R]))
+
+    own = exchange(sent, received.at[1], 6, correct, all_at_once(6))
+    arrive(sent, received.at[1], 6, own)
     owner_sum(received.at[1])
-    own = exchange(back.at[1], result, 7, narrow(back.at[1]))
-    arrive(back.at[1], result, 7, own)
-    save.wait()
-
-
-def extend_kernel(elem, face, coupling, res_inner_h, inner_inv_h, inner_out, face_out, rows, total, terms, res_inner, inner_inv, sems):
-    step = pl.program_id(0)
-    steps = pl.num_programs(0)
-    first = pltpu.make_async_copy(res_inner_h, res_inner, sems.at[0])
-    second = pltpu.make_async_copy(inner_inv_h, inner_inv, sems.at[1])
-
-    @pl.when(step == 0)
-    def _():
-        first.start()
-        second.start()
-
-    def one(i, c):
-        value = unpack(face, step * 16 + i).astype(BF)
-        rows[step * 16 + i] = value
-        terms[i] = jnp.dot(value, coupling[i], preferred_element_type=F32)
+    own = exchange(back, gathered2, 7, narrow(back), in_batches(1))
+
+    def extend(bases, carry):
+        for base in bases:
+            for t in [base + k for k in range(4)]:
+                rows = unpack(gathered2, t).astype(BF)
+                rows_out[t] = rows
+                terms_out[t] = jnp.dot(rows, coupling[t], preferred_element_type=F32)
+        return carry
+
+    arrive_in_batches(back, gathered2, 7, own, in_batches(1), extend, 0)
+
+
+def extend_kernel(
+    elem, rows_h, terms_h, res_inner_h, inner_inv_h, inner_out, face_out,
+    rows, terms, res_inner, total, inner_inv, sems,
+):
+    pairs = ((res_inner_h, res_inner), (terms_h, terms), (rows_h, rows), (inner_inv_h, inner_inv))
+    loads = [pltpu.make_async_copy(src, dst, sems.at[k]) for k, (src, dst) in enumerate(pairs)]
+    for one in loads:
+        one.start()
+    loads[0].wait()
+    total[...] = res_inner[...].astype(F32)
+    loads[1].wait()
+
+    def add(t, c):
+        e = elem[0, t]
+        total[e] = total[e] - terms[t]
         return c
 
-    lax.fori_loop(0, 16, one, 0, unroll=16)
-
-    @pl.when(step == 0)
-    def _():
-        first.wait()
-        total[...] = res_inner[...].astype(F32)
-
-    def add(i, c):
-        e = elem[0, step * 16 + i]
-        total[e] = total[e] - terms[i]
+    lax.fori_loop(0, N, add, 0, unroll=8)
+    loads[2].wait()
+    face_out[...] = jnp.swapaxes(jnp.swapaxes(rows[...], 0, 1), 1, 2)
+    loads[3].wait()
+
+    def inner(e, c):
+        inner_out[e] = rows_times(total[e].astype(BF), inner_inv[e]).astype(BF)
         return c
 
-    lax.fori_loop(0, 16, add, 0, unroll=4)
-
-    @pl.when(step == steps - 1)
-    def _():
-        second.wait()
-
-        def inner(e, c):
-            inner_out[e] = rows_times(total[e].astype(BF), inner_inv[e]).astype(BF)
-            return c
-
-        lax.fori_loop(0, E, inner, 0, unroll=8)
-        face_out[...] = jnp.swapaxes(jnp.swapaxes(rows[...], 0, 1), 1, 2)
+    lax.fori_loop(0, E, inner, 0, unroll=16)
 
 
 def body(
@@ -379,11 +424,11 @@
     sm = pl.BlockSpec(memory_space=pltpu.SMEM)
     slots_last = (1, 2, 0)
     packed = (N, ROWS, 128)
-    result, coupling = pl.pallas_call(
+    rows, terms = pl.pallas_call(
         main_kernel,
-        out_shape=(jax.ShapeDtypeStruct(packed, BF), jax.ShapeDtypeStruct((N, B, B), BF)),
+        out_shape=(jax.ShapeDtypeStruct((N, R, B), BF), jax.ShapeDtypeStruct((N, R, B), F32)),
         in_specs=[hbm] * 7 + [vm] * 3 + [sm],
-        out_specs=(vm, hbm),
+        out_specs=(vm, vm),
         scratch_shapes=[
             pltpu.VMEM((E, R, B), BF),
             pltpu.VMEM((E, B, B), BF),
@@ -401,11 +446,12 @@
             pltpu.VMEM((NCG, GRP * NC), BF),
             pltpu.VMEM((NC, NCG), BF),
             pltpu.VMEM((GRP, 8, 128), jnp.int32),
-            pltpu.VMEM((2, *packed), BF),
+            pltpu.VMEM(packed, BF),
             pltpu.VMEM((2, *packed), BF),
             pltpu.VMEM((N * PITCH, 128), F32),
             pltpu.VMEM((N * PITCH, 128), F32),
-            pltpu.VMEM((2, *packed), BF),
+            pltpu.VMEM(packed, BF),
+            pltpu.VMEM(packed, BF),
             pltpu.VMEM(packed, BF),
             pltpu.VMEM((N, R, B), BF),
             pltpu.VMEM((N, R, B), F32),
@@ -419,6 +465,8 @@
             pltpu.VMEM((N, N), F32),
             pltpu.VMEM((N, N), BF),
             pltpu.SemaphoreType.REGULAR,
+            pltpu.SemaphoreType.DMA((16,)),
+            pltpu.SemaphoreType.DMA((16,)),
             pltpu.SemaphoreType.DMA((8,)),
             pltpu.SemaphoreType.DMA((8,)),
             pltpu.SemaphoreType.DMA((8,)),
@@ -441,30 +489,22 @@
         sharers,
         face_elem,
     )
-    whole = lambda i: (0, 0, 0)
     inner_out, face_out = pl.pallas_call(
         extend_kernel,
-        grid=(N // 16,),
         out_shape=(jax.ShapeDtypeStruct((E, R, B), BF), jax.ShapeDtypeStruct((R, B, N), BF)),
-        in_specs=[
-            sm,
-            pl.BlockSpec(packed, whole),
-            pl.BlockSpec((16, B, B), lambda i: (i, 0, 0)),
-            hbm,
-            hbm,
-        ],
-        out_specs=(pl.BlockSpec((E, R, B), whole), pl.BlockSpec((R, B, N), whole)),
+        in_specs=[sm, hbm, hbm, hbm, hbm],
+        out_specs=(vm, vm),
         scratch_shapes=[
             pltpu.VMEM((N, R, B), BF),
+            pltpu.VMEM((N, R, B), F32),
+            pltpu.VMEM((E, R, B), BF),
             pltpu.VMEM((E, R, B), F32),
-            pltpu.VMEM((16, R, B), F32),
-            pltpu.VMEM((E, R, B), BF),
             pltpu.VMEM((E, B, B), BF),
-            pltpu.SemaphoreType.DMA((2,)),
+            pltpu.SemaphoreType.DMA((4,)),
         ],
         name="extend",
-        compiler_params=pltpu.CompilerParams(vmem_limit_bytes=60 << 20),
-    )(face_elem, result, coupling, res_inner, inner_inv)
+        compiler_params=pltpu.CompilerParams(vmem_limit_bytes=61 << 20),
+    )(face_elem, rows, terms, res_inner, inner_inv)
     return inner_out, jnp.transpose(face_out, (2, 0, 1))
 
 

time: 111 us -> 106 us (0.955)
  Pallas kernels: 110 us -> 105 us
    pallas_call x2, Pallas kernels: 110 us -> 105 us  [the longest x1 98.4 us: body(): pl.pallas_call(main_kernel, out_shape=(jax.ShapeDtypeStruct((N, R, B), BF...]
where the time goes in v4:
time: 106 us
  Pallas kernels  105 us (99%)
    pallas_call x1, Pallas kernels, body(): pl.pallas_call(main_kernel, out_shape=(jax.ShapeDtypeStruct((N, R, B), BF...  98.4 us
    pallas_call x1, Pallas kernels, body(): pl.pallas_call(extend_kernel, out_shape=(jax.ShapeDtypeStruct((E, R, B),...  6.66 us

profile of v4, /device:TPU:1, one launch (start us, length us, event | category | flops | bytes accessed | tf_op | source)
XLA Modules:
  0.0 105.7 jit_solution(16666680625741311561)
XLA Ops:
  0.6 98.4 %assemble_all.1 = (bf16[128,16,144]{2,1,0:T(8,128)(2,1)}, f32[128,16,144]{2,1,0:T(8,128)}) custom-call(bf16[64,16,144]{2,1,0:T(8,128)(2,1)} %res_inner_h.3, bf16[16,144,128]{2,1,0:T(8,128)(2,1)} %bitcast.8, bf16[64,144,144]{2,1,0:T(8,128)(2,1)} %inner_inv_h.3, bf16[144,144,128]{2,1,0:T(8,128)(2,1)} %bitcast.5, bf16[144,144,128]{2,1,0:T(8,128)(2,1)} %bitcast.6, ...), custom_call_target="tpu_custom_call" | custom-call | tf_op jit(solution)/shard_map/assemble_all/pallas_call | solution.py:427
  99.0 6.7 %extend.1 = (bf16[64,16,144]{2,1,0:T(8,128)(2,1)}, bf16[16,144,128]{2,1,0:T(8,128)(2,1)}) custom-call(s32[1,128]{1,0:T(1,128)} %elem.3, bf16[128,16,144]{2,1,0:T(8,128)(2,1)} %get-tuple-element.6.rows_h, f32[128,16,144]{2,1,0:T(8,128)} %get-tuple-element.7.terms_h, bf16[64,16,144]{2,1,0:T(8,128)(2,1)} %res_inner_h.3, bf16[64,144,144]{2,1,0:T(8,128)(2,1)} %inner_inv_h.3), custom_call_target="tpu_custom_call" | custom-call | tf_op jit(solution)/shard_map/extend/pallas_call | solution.py:492

commit v5 on v4

--- a/solution.py
+++ b/solution.py
@@ -31,22 +31,30 @@
     )
 
 
+def put(out, t, rows):
+    out[t] = rows.reshape(ROWS // 2, 2, 128).astype(BF)
+
+
+def get(ref, t):
+    return ref[t].reshape(ROWS, 128).astype(F32)
+
+
 def pack(out, t, value):
-    out[t, 0:R, :] = value[:, 0:128].astype(BF)
     row = lax.broadcasted_iota(jnp.int32, (R, 128), 0)
     lane = lax.broadcasted_iota(jnp.int32, (R, 128), 1)
     tail = jnp.concatenate([value[:, 128:B], jnp.zeros((R, 112), F32)], axis=1)
     for shift in (16, 32, 64):
         tail = tail + pltpu.roll(tail, shift, 1)
     tail = jnp.where((row + lane // 16) % 8 == 0, tail, 0.0)
-    out[t, R:ROWS, :] = jnp.sum(tail.reshape(2, 8, 128), axis=1).astype(BF)
+    tail = jnp.sum(tail.reshape(2, 8, 128), axis=1)
+    put(out, t, jnp.concatenate([value[:, 0:128], tail], axis=0))
 
 
 def unpack(ref, t):
-    tail = ref[t, R:ROWS, :].astype(F32)
-    tail = jnp.broadcast_to(tail[:, None, :], (2, 8, 128)).reshape(R, 128)
+    packed = get(ref, t)
+    tail = jnp.broadcast_to(packed[R:ROWS, None, :], (2, 8, 128)).reshape(R, 128)
     tail = pltpu.roll(tail, 0, 1, stride=16, stride_axis=0)
-    return jnp.concatenate([ref[t, 0:R, :].astype(F32), tail[:, 0:16]], axis=1)
+    return jnp.concatenate([packed[0:R], tail[:, 0:16]], axis=1)
 
 
 def pieces(x):
@@ -68,12 +76,12 @@
 def main_kernel(
     res_inner_h, res_face_h, inner_inv_h, coupling_h, face_inv_h, basis_h, coarse_inv_h,
     map_row_own, index_row, sharers, elem,
-    rows_out, terms_out,
+    rows_h, terms_h,
     res_inner, inner_inv, inner_w, res_face, face_rows, stage, coupling, face_inv, basis_stage, basis,
     coarse_inv, coarse_high, coarse_low, pick, own_pick, maps,
     sent, received, wide, wide2, back, gathered, gathered2, restricted, local,
     part, part_in, share, share_in, chosen, chosen_in, map_block, weight, contrast,
-    entered, piece_sems, batch_sems, load_sems, send_sems, recv_sems, own_sems,
+    rows_out, terms_out, out_sems, entered, piece_sems, batch_sems, load_sems, send_sems, recv_sems, own_sems,
 ):
     sub = lax.axis_index("sub")
     grp = lax.axis_index("grp")
@@ -240,14 +248,14 @@
 
     own = exchange(sent, received.at[0], 1, condense, all_at_once(1))
     load(face_inv_h, stage, 6).wait()
-    turns(stage, face_inv, 0, 4)
+    turns(stage, face_inv, 0, 8)
     arrive(sent, received.at[0], 1, own)
 
     same = contrast[...]
 
     def owner_sum(source):
         def widen(s):
-            wide[pl.ds(pl.multiple_of(s * PITCH, 8), ROWS)] = source[s].astype(F32)
+            wide[pl.ds(pl.multiple_of(s * PITCH, 8), ROWS)] = get(source, s)
 
         each(0, N, widen, 8)
         for k in range(ROWS):
@@ -257,14 +265,14 @@
     def narrow(target):
         def one(base):
             for t in [base + k for k in range(4)]:
-                target[t] = wide2[pl.ds(pl.multiple_of(t * PITCH, 8), ROWS)].astype(BF)
+                put(target, t, wide2[pl.ds(pl.multiple_of(t * PITCH, 8), ROWS)])
 
         return one
 
     owner_sum(received.at[0])
     own = exchange(back, gathered, 2, narrow(back), in_batches(0))
 
-    turns(stage, face_inv, 4, 9)
+    turns(stage, face_inv, 8, 9)
     load(basis_h, basis_stage, 4).wait()
     turns(basis_stage, basis, 0, 4)
     load(coarse_inv_h, coarse_inv, 5).wait()
@@ -381,9 +389,15 @@
                 rows = unpack(gathered2, t).astype(BF)
                 rows_out[t] = rows
                 terms_out[t] = jnp.dot(rows, coupling[t], preferred_element_type=F32)
+        for base in bases:
+            four = pl.ds(base, 4)
+            pltpu.make_async_copy(rows_out.at[four], rows_h.at[four], out_sems.at[0]).start()
+            pltpu.make_async_copy(terms_out.at[four], terms_h.at[four], out_sems.at[1]).start()
         return carry
 
     arrive_in_batches(back, gathered2, 7, own, in_batches(1), extend, 0)
+    pltpu.make_async_copy(rows_out, rows_h, out_sems.at[0]).wait()
+    pltpu.make_async_copy(terms_out, terms_h, out_sems.at[1]).wait()
 
 
 def extend_kernel(
@@ -423,12 +437,12 @@
     hbm = pl.BlockSpec(memory_space=pl.ANY)
     sm = pl.BlockSpec(memory_space=pltpu.SMEM)
     slots_last = (1, 2, 0)
-    packed = (N, ROWS, 128)
+    packed = (N, ROWS // 2, 2, 128)
     rows, terms = pl.pallas_call(
         main_kernel,
         out_shape=(jax.ShapeDtypeStruct((N, R, B), BF), jax.ShapeDtypeStruct((N, R, B), F32)),
         in_specs=[hbm] * 7 + [vm] * 3 + [sm],
-        out_specs=(vm, vm),
+        out_specs=(hbm, hbm),
         scratch_shapes=[
             pltpu.VMEM((E, R, B), BF),
             pltpu.VMEM((E, B, B), BF),
@@ -464,6 +478,9 @@
             pltpu.VMEM((8, 128), jnp.int32),
             pltpu.VMEM((N, N), F32),
             pltpu.VMEM((N, N), BF),
+            pltpu.VMEM((N, R, B), BF),
+            pltpu.VMEM((N, R, B), F32),
+            pltpu.SemaphoreType.DMA((2,)),
             pltpu.SemaphoreType.REGULAR,
             pltpu.SemaphoreType.DMA((16,)),
             pltpu.SemaphoreType.DMA((16,)),

time: 106 us -> 97.5 us (0.920)
  Pallas kernels: 105 us -> 96.7 us
    pallas_call x1, Pallas kernels: 98.4 us -> 90.1 us  [body(): pl.pallas_call(main_kernel, out_shape=(jax.ShapeDtypeStruct((N, R, B), BF...]
where the time goes in v5:
time: 97.5 us; the launch traced here: 97.4 us
  Pallas kernels  96.7 us (99%)
    pallas_call x1, Pallas kernels, body(): pl.pallas_call(main_kernel, out_shape=(jax.ShapeDtypeStruct((N, R, B), BF...  90.1 us
    pallas_call x1, Pallas kernels, body(): pl.pallas_call(extend_kernel, out_shape=(jax.ShapeDtypeStruct((E, R, B),...  6.66 us

profile of v5, /device:TPU:1, one launch (start us, length us, event | category | flops | bytes accessed | tf_op | source)
XLA Modules:
  0.0 97.4 jit_solution(5888826715131629161)
XLA Ops:
  0.6 90.1 %assemble_all.1 = (bf16[128,16,144]{2,1,0:T(8,128)(2,1)}, f32[128,16,144]{2,1,0:T(8,128)}) custom-call(bf16[64,16,144]{2,1,0:T(8,128)(2,1)} %res_inner_h.3, bf16[16,144,128]{2,1,0:T(8,128)(2,1)} %bitcast.8, bf16[64,144,144]{2,1,0:T(8,128)(2,1)} %inner_inv_h.3, bf16[144,144,128]{2,1,0:T(8,128)(2,1)} %bitcast.5, bf16[144,144,128]{2,1,0:T(8,128)(2,1)} %bitcast.6, ...), custom_call_target="tpu_custom_call" | custom-call | tf_op jit(solution)/shard_map/assemble_all/pallas_call | solution.py:441
  90.7 6.7 %extend.1 = (bf16[64,16,144]{2,1,0:T(8,128)(2,1)}, bf16[16,144,128]{2,1,0:T(8,128)(2,1)}) custom-call(s32[1,128]{1,0:T(1,128)} %elem.3, bf16[128,16,144]{2,1,0:T(8,128)(2,1)} %get-tuple-element.6.rows_h, f32[128,16,144]{2,1,0:T(8,128)} %get-tuple-element.7.terms_h, bf16[64,16,144]{2,1,0:T(8,128)(2,1)} %res_inner_h.3, bf16[64,144,144]{2,1,0:T(8,128)(2,1)} %inner_inv_h.3), custom_call_target="tpu_custom_call" | custom-call | tf_op jit(solution)/shard_map/extend/pallas_call | solution.py:509

commit v6 on v5

--- a/solution.py
+++ b/solution.py
@@ -103,11 +103,11 @@
     def coupling_piece(q):
         return piece(coupling_h, stage, q, 4)
 
+    for q in range(9):
+        coupling_piece(q).start()
     for q in range(4):
         inverse_piece(q).start()
     load(res_face_h, res_face, 3).start()
-    for q in range(9):
-        coupling_piece(q).start()
 
     def signal(semaphore, device):
         pl.semaphore_signal(semaphore, inc=1, device_id=device, device_id_type=MESH)
@@ -132,6 +132,27 @@
     index = index_row[...].astype(F32)
     contrast[...] = jnp.where((index == tall(index)) & (index < 32.0), 1.0, 0.0).astype(BF)
 
+    def turn(src, dst, q):
+        part_rows = src[pl.ds(pl.multiple_of(q * 16, 16), 16)]
+        part_rows = jnp.swapaxes(jnp.swapaxes(part_rows, 1, 2), 0, 1)
+        dst[:, pl.ds(pl.multiple_of(q * 16, 16), 16), :] = part_rows
+
+    def turns(src, dst, first, last):
+        def one(q, c):
+            turn(src, dst, q)
+            return c
+
+        lax.fori_loop(first, last, one, 0)
+
+    def coupling_turn(q):
+        coupling_piece(q).wait()
+        turn(stage, coupling, q)
+
+    each(0, 9, coupling_turn)
+    load(face_inv_h, stage, 6).start()
+    pl.semaphore_wait(barrier, GRP + SUB - 2)
+    each(1, SUB, lambda i: signal(entered, (lax.rem(sub + i, SUB), grp)))
+
     def inner(e):
         inner_w[e] = rows_times(res_inner[e], inner_inv[e]).astype(BF)
 
@@ -143,33 +164,10 @@
             inner(16 * q + e)
 
     each(0, 4, inners)
-    pl.semaphore_wait(barrier, GRP + SUB - 2)
-    each(1, SUB, lambda i: signal(entered, (lax.rem(sub + i, SUB), grp)))
-
-    def turn(src, dst, q):
-        part_rows = src[pl.ds(pl.multiple_of(q * 16, 16), 16)]
-        part_rows = jnp.swapaxes(jnp.swapaxes(part_rows, 1, 2), 0, 1)
-        dst[:, pl.ds(pl.multiple_of(q * 16, 16), 16), :] = part_rows
-
-    def turns(src, dst, first, last):
-        def one(q, c):
-            turn(src, dst, q)
-            return c
-
-        lax.fori_loop(first, last, one, 0)
-
+    load(basis_h, basis_stage, 4).start()
+    load(coarse_inv_h, coarse_inv, 5).start()
     load(res_face_h, res_face, 3).wait()
     turns(res_face, face_rows, 0, 1)
-
-    def coupling_turn(q):
-        coupling_piece(q).wait()
-        turn(stage, coupling, q)
-
-    each(0, 9, coupling_turn)
-    load(face_inv_h, stage, 6).start()
-    load(basis_h, basis_stage, 4).start()
-    load(coarse_inv_h, coarse_inv, 5).start()
-
     pl.semaphore_wait(entered, SUB - 1)
 
     def map_copy(i):
@@ -182,25 +180,27 @@
     def quad(i):
         return lax.rem(me // 4 + i, N // 4) * 4
 
-    def exchange(source, target, k, fill, arrived):
-        def give(t, q):
-            remote(source.at[t], target.at[me], place(t), send_sems.at[k], arrived(q)).start()
+    def exchange(source, target, k, fill, arrived, size):
+        def give(t, j):
+            remote(source.at[t], target.at[me], place(t), send_sems.at[k], arrived(j // 16)).start()
 
         def batch(q):
-            for i in range(4):
-                fill(quad(q * 4 + i))
+            for i in range(size // 4):
+                fill(quad(q * (size // 4) + i))
+
+        def pass_on(j):
+            give(quad(j // 4) + lax.rem(me + j, 4), j)
 
         batch(0)
         own = pltpu.make_async_copy(source.at[me], target.at[me], own_sems.at[k])
         own.start()
-        each(1, 4, lambda j: give(quad(0) + lax.rem(me + j, 4), 0))
-        each(4, 16, lambda j: give(quad(j // 4) + lax.rem(me + j, 4), 0))
+        each(1, size, pass_on)
 
         def more(q):
             batch(q)
-            each(16 * q, 16 * q + 16, lambda j: give(quad(j // 4) + lax.rem(me + j, 4), q))
-
-        each(1, N // 16, more)
+            each(size * q, size * q + size, pass_on)
+
+        each(1, N // size, more)
         return own
 
     def all_at_once(k):
@@ -246,7 +246,7 @@
             product = rows_times(inner_w[elem[0, t]], coupling[t])
             pack(sent, t, scaled(t, face_rows[t].astype(F32) - product))
 
-    own = exchange(sent, received.at[0], 1, condense, all_at_once(1))
+    own = exchange(sent, received.at[0], 1, condense, all_at_once(1), 32)
     load(face_inv_h, stage, 6).wait()
     turns(stage, face_inv, 0, 8)
     arrive(sent, received.at[0], 1, own)
@@ -270,7 +270,7 @@
         return one
 
     owner_sum(received.at[0])
-    own = exchange(back, gathered, 2, narrow(back), in_batches(0))
+    own = exchange(back, gathered, 2, narrow(back), in_batches(0), 16)
 
     turns(stage, face_inv, 8, 9)
     load(basis_h, basis_stage, 4).wait()
@@ -337,7 +337,7 @@
         local[t] = rows_times(restricted[t], face_inv[t])
 
     ring_send(part, part_in, 3)
-    each(0, 64, solve_local, 8)
+    each(0, 64, solve_local, 32)
     own.wait()
     ring_wait(part, part_in, 3)
     share[...] = jnp.sum(part_in[...], axis=0)
@@ -349,7 +349,7 @@
         remote(share, share_in.at[sub], (t, grp), send_sems.at[4], recv_sems.at[4]).start()
 
     each(1, SUB, share_copy)
-    each(64, N, solve_local, 8)
+    each(64, N, solve_local, 32)
     own.wait()
     fifteen = pl.ds(0, SUB - 1)
     remote(share_in.at[fifteen], share_in.at[fifteen], (sub, grp), send_sems.at[4], recv_sems.at[4]).wait()
@@ -378,10 +378,10 @@
         for k in range(4):
             pack(sent, base + k, scaled(base + k, local[base + k] + coarse[k * R : (k + 1) * R]))
 
-    own = exchange(sent, received.at[1], 6, correct, all_at_once(6))
+    own = exchange(sent, received.at[1], 6, correct, all_at_once(6), 32)
     arrive(sent, received.at[1], 6, own)
     owner_sum(received.at[1])
-    own = exchange(back, gathered2, 7, narrow(back), in_batches(1))
+    own = exchange(back, gathered2, 7, narrow(back), in_batches(1), 16)
 
     def extend(bases, carry):
         for base in bases:
@@ -426,7 +426,7 @@
         inner_out[e] = rows_times(total[e].astype(BF), inner_inv[e]).astype(BF)
         return c
 
-    lax.fori_loop(0, E, inner, 0, unroll=16)
+    lax.fori_loop(0, E, inner, 0, unroll=32)
 
 
 def body(

time: 97.5 us -> 94.3 us (0.967)
  Pallas kernels: 96.7 us -> 93.6 us
    pallas_call x1, Pallas kernels: 90.1 us -> 87.1 us  [body(): pl.pallas_call(main_kernel, out_shape=(jax.ShapeDtypeStruct((N, R, B), BF...]
where the time goes in v6:
time: 94.3 us; the launch traced here: 94.2 us
  Pallas kernels  93.6 us (99%)
    pallas_call x1, Pallas kernels, body(): pl.pallas_call(main_kernel, out_shape=(jax.ShapeDtypeStruct((N, R, B), BF...  87.1 us
    pallas_call x1, Pallas kernels, body(): pl.pallas_call(extend_kernel, out_shape=(jax.ShapeDtypeStruct((E, R, B),...  6.43 us

profile of v6, /device:TPU:1, one launch (start us, length us, event | category | flops | bytes accessed | tf_op | source)
XLA Modules:
  0.0 94.2 jit_solution(17924318391574275288)
XLA Ops:
  0.6 87.1 %assemble_all.1 = (bf16[128,16,144]{2,1,0:T(8,128)(2,1)}, f32[128,16,144]{2,1,0:T(8,128)}) custom-call(bf16[64,16,144]{2,1,0:T(8,128)(2,1)} %res_inner_h.3, bf16[16,144,128]{2,1,0:T(8,128)(2,1)} %bitcast.8, bf16[64,144,144]{2,1,0:T(8,128)(2,1)} %inner_inv_h.3, bf16[144,144,128]{2,1,0:T(8,128)(2,1)} %bitcast.5, bf16[144,144,128]{2,1,0:T(8,128)(2,1)} %bitcast.6, ...), custom_call_target="tpu_custom_call" | custom-call | tf_op jit(solution)/shard_map/assemble_all/pallas_call | solution.py:441
  87.8 6.4 %extend.1 = (bf16[64,16,144]{2,1,0:T(8,128)(2,1)}, bf16[16,144,128]{2,1,0:T(8,128)(2,1)}) custom-call(s32[1,128]{1,0:T(1,128)} %elem.3, bf16[128,16,144]{2,1,0:T(8,128)(2,1)} %get-tuple-element.6.rows_h, f32[128,16,144]{2,1,0:T(8,128)} %get-tuple-element.7.terms_h, bf16[64,16,144]{2,1,0:T(8,128)(2,1)} %res_inner_h.3, bf16[64,144,144]{2,1,0:T(8,128)(2,1)} %inner_inv_h.3), custom_call_target="tpu_custom_call" | custom-call | tf_op jit(solution)/shard_map/extend/pallas_call | solution.py:509

commit v7 on v6

--- a/solution.py
+++ b/solution.py
@@ -248,7 +248,9 @@
 
     own = exchange(sent, received.at[0], 1, condense, all_at_once(1), 32)
     load(face_inv_h, stage, 6).wait()
-    turns(stage, face_inv, 0, 8)
+    load(basis_h, basis_stage, 4).wait()
+    turns(basis_stage, basis, 0, 4)
+    turns(stage, face_inv, 0, 5)
     arrive(sent, received.at[0], 1, own)
 
     same = contrast[...]
@@ -272,9 +274,7 @@
     owner_sum(received.at[0])
     own = exchange(back, gathered, 2, narrow(back), in_batches(0), 16)
 
-    turns(stage, face_inv, 8, 9)
-    load(basis_h, basis_stage, 4).wait()
-    turns(basis_stage, basis, 0, 4)
+    turns(stage, face_inv, 5, 9)
     load(coarse_inv_h, coarse_inv, 5).wait()
 
     def split(q):

time: 94.3 us -> 94.3 us (level)
  no operation moved by 1% of the time
where the time goes in v7:
time: 94.3 us; the launch traced here: 94.2 us
  Pallas kernels  93.6 us (99%)
    pallas_call x1, Pallas kernels, body(): pl.pallas_call(main_kernel, out_shape=(jax.ShapeDtypeStruct((N, R, B), BF...  87.1 us
    pallas_call x1, Pallas kernels, body(): pl.pallas_call(extend_kernel, out_shape=(jax.ShapeDtypeStruct((E, R, B),...  6.43 us

profile of v7, /device:TPU:1, one launch (start us, length us, event | category | flops | bytes accessed | tf_op | source)
XLA Modules:
  0.0 94.2 jit_solution(10350350250138937202)
XLA Ops:
  0.6 87.1 %assemble_all.1 = (bf16[128,16,144]{2,1,0:T(8,128)(2,1)}, f32[128,16,144]{2,1,0:T(8,128)}) custom-call(bf16[64,16,144]{2,1,0:T(8,128)(2,1)} %res_inner_h.3, bf16[16,144,128]{2,1,0:T(8,128)(2,1)} %bitcast.8, bf16[64,144,144]{2,1,0:T(8,128)(2,1)} %inner_inv_h.3, bf16[144,144,128]{2,1,0:T(8,128)(2,1)} %bitcast.5, bf16[144,144,128]{2,1,0:T(8,128)(2,1)} %bitcast.6, ...), custom_call_target="tpu_custom_call" | custom-call | tf_op jit(solution)/shard_map/assemble_all/pallas_call | solution.py:441
  87.8 6.4 %extend.1 = (bf16[64,16,144]{2,1,0:T(8,128)(2,1)}, bf16[16,144,128]{2,1,0:T(8,128)(2,1)}) custom-call(s32[1,128]{1,0:T(1,128)} %elem.3, bf16[128,16,144]{2,1,0:T(8,128)(2,1)} %get-tuple-element.6.rows_h, f32[128,16,144]{2,1,0:T(8,128)} %get-tuple-element.7.terms_h, bf16[64,16,144]{2,1,0:T(8,128)(2,1)} %res_inner_h.3, bf16[64,144,144]{2,1,0:T(8,128)(2,1)} %inner_inv_h.3), custom_call_target="tpu_custom_call" | custom-call | tf_op jit(solution)/shard_map/extend/pallas_call | solution.py:509
